TPU v7x, 128 devices: a whole 4x4x4 slice. The times are simulated.
128 devices in a mesh: dp: 32 (over x, z, y_lo), tensor: 4 (over y_hi, core).
Axes of the slice: x: 4, y: 4 (y_hi: 2, y_lo: 2; y = y_hi * 2 + y_lo), z: 4, core: 2. Of those that a mesh axis runs over, the one named last changes fastest.
Arguments:
- tokens: bfloat16 [32768, 1024], P(('dp', 'tensor')), may hold values from -24 to 24
- cotangent: bfloat16 [32768, 1024], P(('dp', 'tensor')), may hold values from -24 to 24
- segments: int32 [32768], P('dp'), may hold values from 0 to 3, as said below
- ln1_gain: bfloat16 [1024], P('dp'), may hold values from 0.5 to 1.5
- ln1_bias: bfloat16 [1024], P('dp'), may hold values from -1.25 to 1.25
- w_qkv: bfloat16 [1024, 3, 1024], P('dp', None, 'tensor'), may hold values from -0.1875 to 0.1875
- bias_qv: bfloat16 [2, 16, 64], P(None, 'tensor', 'dp'), may hold values from -1.75 to 1.75
- w_out: bfloat16 [1024, 1024], P('tensor', 'dp'), may hold values from -0.375 to 0.375
- bias_out: bfloat16 [1024], P('dp'), may hold values from -1.25 to 1.25
- ln2_gain: bfloat16 [1024], P('dp'), may hold values from 0.5 to 1.5
- ln2_bias: bfloat16 [1024], P('dp'), may hold values from -1.25 to 1.25
- w_fc: bfloat16 [1024, 4096], P('dp', 'tensor'), may hold values from -0.1875 to 0.1875
- bias_fc: bfloat16 [32, 128], P('tensor', 'dp'), may hold values from -1.75 to 1.75
- w_proj: bfloat16 [4096, 1024], P('tensor', 'dp'), may hold values from -0.09375 to 0.09375
- bias_proj: bfloat16 [1024], P('dp'), may hold values from -1.25 to 1.25
Outputs:
- mixed: bfloat16 [32768, 1024], P(('dp', 'tensor'))
- input_grad: float32 [32768, 1024], P(('dp', 'tensor'))
- grad_ln1_gain: float32 [1024], P(('dp', 'tensor'))
- grad_ln1_bias: float32 [1024], P(('dp', 'tensor'))
- grad_qkv: float32 [1024, 3, 1024], P('dp', None, 'tensor')
- grad_bias_qv: float32 [2, 16, 64], P(None, 'tensor', 'dp')
- grad_out: float32 [1024, 1024], P('tensor', 'dp')
- grad_bias_out: float32 [1024], P('dp')
- grad_ln2_gain: float32 [1024], P(('dp', 'tensor'))
- grad_ln2_bias: float32 [1024], P(('dp', 'tensor'))
- grad_fc: float32 [1024, 4096], P('dp', 'tensor')
- grad_bias_fc: float32 [32, 128], P('tensor', 'dp')
- grad_proj: float32 [4096, 1024], P('tensor', 'dp')
- grad_bias_proj: float32 [1024], P('dp')
Inputs may be any that keep to these rules, and one draw needn't show every extreme that they name: `segments`: within each sequence of 1024 tokens the numbers start at 0, never fall and rise by one at three document bounds; the second document begins within the first 128 tokens and ends within the last 128.
All inputs are finite; a program needn't handle non-finite values.
Results may differ from a plain program's by a relative error of at most 0.014.
Values may be sent and summed in bfloat16 or wider, within the bound.
No kernel may reach another device: no remote copies, remote signals or barrier semaphores. Data moves between devices by JAX's collectives and lax.ppermute only.
A program may use at most 128 MiB of HBM per device.

v0:
```python
import math

import jax
import jax.numpy as jnp
from jax import lax
from jax.sharding import PartitionSpec as P

HD = 64
SEQ = 1024


def side_by_side(arrays, axis, dim, along):
    widths = [math.prod(a.shape[along:]) for a in arrays]
    both = jnp.concatenate(
        [a.reshape(*a.shape[:along], w) for a, w in zip(arrays, widths)], axis=along
    )
    out = lax.all_gather(both, axis, axis=dim, tiled=True)
    parts = jnp.split(out, [sum(widths[:k]) for k in range(1, len(widths))], axis=along)
    return tuple((b.reshape(*out.shape[:along], *a.shape[along:]) for a, b in zip(arrays, parts)))


def sent_to_all(shard, axis):
    copies = jnp.broadcast_to(shard, (lax.axis_size(axis), *shard.shape))
    return lax.all_to_all(copies, axis, split_axis=0, concat_axis=0, tiled=True)


def joined_along(parts, dim):
    shape = list(parts.shape[1:])
    shape[dim] *= parts.shape[0]
    return jnp.moveaxis(parts, 0, dim).reshape(shape)


def gather_directly(shard, axis, dim):
    parts = sent_to_all(shard, axis)
    return joined_along(parts, dim)


def cut_along(shard, dim, devices):
    shape = shard.shape
    parts = shard.reshape(*shape[:dim], devices, shape[dim] // devices, *shape[dim + 1 :])
    return jnp.moveaxis(parts, dim, 0)


def summed_on_arrival(shard, axis, dim):
    devices = lax.axis_size(axis)
    parts = lax.all_to_all(cut_along(shard, dim, devices), axis, 0, 0, tiled=True)
    return jnp.sum(parts, axis=0)


def sent_together(arrays, axis, dim, along):
    columns = [a.reshape(*a.shape[:along], -1) for a in arrays]
    both = jnp.concatenate(columns, axis=along)
    out, at, done = (lax.psum_scatter(both, axis, scatter_dimension=dim, tiled=True), 0, [])
    for a, column in zip(arrays, columns):
        share = out[..., at : at + column.shape[along]]
        done.append(share.reshape(*share.shape[:along], *a.shape[along:]))
        at += column.shape[along]
    return tuple(done)


def layer_norm(values, scales, offsets):
    centered = values - jnp.mean(values, axis=-1, keepdims=True)
    variance = jnp.mean(centered * centered, axis=-1, keepdims=True)
    return centered * lax.rsqrt(variance + 1e-05) * scales + offsets


def smooth_gate(values):
    return jax.nn.gelu(values, approximate=True)


def inner_rows(left_side, right_side):
    return lax.dot_general(
        left_side, right_side, (((0,), (0,)), ((), ())), preferred_element_type=jnp.float32
    )


def outer_cols(left_side, right_side):
    return lax.dot_general(
        left_side, right_side, (((1,), (1,)), ((), ())), preferred_element_type=jnp.float32
    )


def score_block(query_rows, key_rows, label_rows, labels, offset_row):
    raw_scores = jnp.einsum(
        "qhd,khd->hqk", query_rows, key_rows, preferred_element_type=jnp.float32
    ) * HD ** (-0.5)
    row_places = offset_row + jnp.arange(query_rows.shape[0], dtype=jnp.int32)
    key_places = jnp.arange(key_rows.shape[0], dtype=jnp.int32)
    allowed = (label_rows[:, None] == labels[None, :]) & (
        key_places[None, :] <= row_places[:, None]
    )
    return jnp.where(allowed[None], raw_scores, -1e30)


def attend_forward(joined_rows, labels, head_width):
    seq_total = joined_rows.shape[0] // SEQ
    heads_local = head_width // HD
    block_rows = min(512, SEQ)
    block_count = SEQ // block_rows
    split_view = joined_rows.reshape(seq_total, SEQ, 3, heads_local, HD)
    label_view = labels.reshape(seq_total, SEQ)

    def one_block(number):
        chosen = number // block_count
        offset_row = number % block_count * block_rows
        whole_seq = split_view[chosen]
        label_all = label_view[chosen]
        query_rows = lax.dynamic_slice_in_dim(whole_seq[:, 0], offset_row, block_rows, 0)
        label_rows = lax.dynamic_slice_in_dim(label_all, offset_row, block_rows, 0)
        scores = score_block(query_rows, whole_seq[:, 1], label_rows, label_all, offset_row)
        highest = jnp.max(scores, axis=-1, keepdims=True)
        expanded = jnp.exp(scores - highest)
        totals = jnp.sum(expanded, axis=-1, keepdims=True)
        probable = (expanded / totals).astype(jnp.bfloat16)
        context = jnp.einsum(
            "hqk,khd->qhd", probable, whole_seq[:, 2], preferred_element_type=jnp.float32
        )
        return (context.astype(jnp.bfloat16), (highest + jnp.log(totals))[..., 0])

    context, log_totals = lax.map(one_block, jnp.arange(seq_total * block_count, dtype=jnp.int32))
    return (context.reshape(seq_total * SEQ, head_width), log_totals)


def attend_backward(joined_rows, d_context, log_totals, labels, head_width):
    seq_total = joined_rows.shape[0] // SEQ
    heads_local = head_width // HD
    block_rows = min(512, SEQ)
    block_count = SEQ // block_rows
    split_view = joined_rows.reshape(seq_total, SEQ, 3, heads_local, HD)
    label_view = labels.reshape(seq_total, SEQ)
    d_view = d_context.reshape(seq_total, SEQ, heads_local, HD)
    scale_factor = HD ** (-0.5)

    def one_block(pieces):
        number, log_rows = pieces
        chosen = number // block_count
        offset_row = number % block_count * block_rows
        whole_seq = split_view[chosen]
        label_all = label_view[chosen]
        key_all = whole_seq[:, 1]
        value_all = whole_seq[:, 2]
        query_rows = lax.dynamic_slice_in_dim(whole_seq[:, 0], offset_row, block_rows, 0)
        label_rows = lax.dynamic_slice_in_dim(label_all, offset_row, block_rows, 0)
        d_rows = lax.dynamic_slice_in_dim(d_view[chosen], offset_row, block_rows, 0)
        scores = score_block(query_rows, key_all, label_rows, label_all, offset_row)
        probs_full = jnp.exp(scores - log_rows[..., None])
        probable = probs_full.astype(jnp.bfloat16)
        d_probs = jnp.einsum("qhd,khd->hqk", d_rows, value_all, preferred_element_type=jnp.float32)
        d_values = jnp.einsum("hqk,qhd->khd", probable, d_rows, preferred_element_type=jnp.float32)
        d_scores = (
            probs_full * (d_probs - jnp.sum(probs_full * d_probs, axis=-1, keepdims=True))
        ).astype(jnp.bfloat16)
        d_queries = (
            jnp.einsum("hqk,khd->qhd", d_scores, key_all, preferred_element_type=jnp.float32)
            * scale_factor
        )
        d_keys = (
            jnp.einsum("hqk,qhd->khd", d_scores, query_rows, preferred_element_type=jnp.float32)
            * scale_factor
        )
        return (d_queries.astype(jnp.bfloat16), d_keys, d_values)

    d_queries, d_keys, d_values = lax.map(
        one_block, (jnp.arange(seq_total * block_count, dtype=jnp.int32), log_totals)
    )
    d_queries = d_queries.reshape(seq_total, SEQ, heads_local, HD)
    d_keys = jnp.sum(d_keys.reshape(seq_total, block_count, SEQ, heads_local, HD), axis=1).astype(
        jnp.bfloat16
    )
    d_values = jnp.sum(
        d_values.reshape(seq_total, block_count, SEQ, heads_local, HD), axis=1
    ).astype(jnp.bfloat16)
    return jnp.stack([d_queries, d_keys, d_values], axis=2).reshape(seq_total * SEQ, 3 * head_width)


def shards(
    tokens,
    cotangent,
    segments,
    ln1_gain,
    ln1_bias,
    w_qkv,
    bias_qv,
    w_out,
    bias_out,
    ln2_gain,
    ln2_bias,
    w_fc,
    bias_fc,
    w_proj,
    bias_proj,
):
    gain_one, shift_one, qkv_all, qv_bias_all, out_all, out_bias_all = (
        lax.all_gather(ln1_gain, "dp", axis=0, tiled=True),
        *side_by_side((ln1_bias, w_qkv), "dp", 0, 1),
        lax.all_gather(bias_qv, "dp", axis=2, tiled=True),
        lax.all_gather(w_out, "dp", axis=1, tiled=True),
        lax.all_gather(bias_out, "dp", axis=0, tiled=True),
    )
    gain_two, shift_two, fc_all, fc_bias_all, proj_all, proj_bias_all = (
        lax.all_gather(ln2_gain, "dp", axis=0, tiled=True),
        *side_by_side((ln2_bias, w_fc), "dp", 0, 1),
        lax.all_gather(bias_fc, "dp", axis=1, tiled=True),
        lax.all_gather(w_proj, "dp", axis=1, tiled=True),
        lax.all_gather(bias_proj, "dp", axis=0, tiled=True),
    )
    model_width = qkv_all.shape[0]
    head_width = qkv_all.shape[2]
    qkv_flat = qkv_all.reshape(model_width, 3 * head_width)
    inputs = tokens.astype(jnp.float32)
    normed_one, pull_one = jax.vjp(
        layer_norm, inputs, gain_one.astype(jnp.float32), shift_one.astype(jnp.float32)
    )
    rows_one = gather_directly(normed_one.astype(jnp.bfloat16), "tensor", 0)
    bias_row = jnp.concatenate(
        [
            qv_bias_all[0].reshape(head_width),
            jnp.zeros((head_width,), jnp.bfloat16),
            qv_bias_all[1].reshape(head_width),
        ]
    ).astype(jnp.float32)
    joined_rows = (
        jnp.dot(rows_one, qkv_flat, preferred_element_type=jnp.float32) + bias_row
    ).astype(jnp.bfloat16)
    context, log_totals = attend_forward(joined_rows, segments, head_width)
    attn_piece = summed_on_arrival(
        jnp.dot(context, out_all, preferred_element_type=jnp.float32), "tensor", 0
    )
    middle = inputs + attn_piece + out_bias_all.astype(jnp.float32)
    normed_two, pull_two = jax.vjp(
        layer_norm, middle, gain_two.astype(jnp.float32), shift_two.astype(jnp.float32)
    )
    rows_two = gather_directly(normed_two.astype(jnp.bfloat16), "tensor", 0)
    hidden = jnp.dot(rows_two, fc_all, preferred_element_type=jnp.float32) + fc_bias_all.reshape(
        -1
    ).astype(jnp.float32)
    activated, pull_gate = jax.vjp(smooth_gate, hidden)
    active_low = activated.astype(jnp.bfloat16)
    mlp_piece = summed_on_arrival(
        jnp.dot(active_low, proj_all, preferred_element_type=jnp.float32), "tensor", 0
    )
    mixed = (middle + mlp_piece + proj_bias_all.astype(jnp.float32)).astype(jnp.bfloat16)
    cot_all = gather_directly(cotangent, "tensor", 0)
    grad_proj_bias = jnp.sum(cot_all, axis=0, dtype=jnp.float32)
    grad_proj = inner_rows(active_low, cot_all)
    (d_hidden,) = pull_gate(outer_cols(cot_all, proj_all))
    d_hidden_low = d_hidden.astype(jnp.bfloat16)
    grad_fc = inner_rows(rows_two, d_hidden_low)
    grad_fc_bias = jnp.sum(d_hidden_low, axis=0, dtype=jnp.float32).reshape(fc_bias_all.shape)
    d_normed_two = summed_on_arrival(outer_cols(d_hidden_low, fc_all), "tensor", 0)
    d_middle_norm, grad_gain_two, grad_shift_two = pull_two(d_normed_two)
    d_middle = cotangent.astype(jnp.float32) + d_middle_norm
    d_mid_all = gather_directly(d_middle.astype(jnp.bfloat16), "tensor", 0)
    grad_out_bias = jnp.sum(d_mid_all, axis=0, dtype=jnp.float32)
    grad_out = inner_rows(context, d_mid_all)
    d_context = outer_cols(d_mid_all, out_all).astype(jnp.bfloat16)
    d_joined = attend_backward(joined_rows, d_context, log_totals, segments, head_width)
    grad_qkv = inner_rows(rows_one, d_joined).reshape(model_width, 3, head_width)
    joined_view = d_joined.reshape(-1, 3, head_width)
    grad_bias_qv = jnp.stack(
        [
            jnp.sum(joined_view[:, 0], axis=0, dtype=jnp.float32),
            jnp.sum(joined_view[:, 2], axis=0, dtype=jnp.float32),
        ]
    ).reshape(qv_bias_all.shape)
    d_normed_one = summed_on_arrival(outer_cols(d_joined, qkv_flat), "tensor", 0)
    d_input_norm, grad_gain_one, grad_shift_one = pull_one(d_normed_one)
    input_grad = d_middle + d_input_norm
    norm_shares = lax.psum_scatter(
        jnp.stack([grad_gain_one, grad_shift_one, grad_gain_two, grad_shift_two]),
        ("dp", "tensor"),
        scatter_dimension=1,
        tiled=True,
    )
    all_shares = (
        lax.psum_scatter(grad_qkv, "dp", scatter_dimension=0, tiled=True),
        lax.psum_scatter(grad_bias_qv, "dp", scatter_dimension=2, tiled=True),
        lax.psum_scatter(grad_out, "dp", scatter_dimension=1, tiled=True),
        *sent_together((grad_out_bias, grad_fc), "dp", 0, 1),
        lax.psum_scatter(grad_fc_bias, "dp", scatter_dimension=1, tiled=True),
        lax.psum_scatter(grad_proj, "dp", scatter_dimension=1, tiled=True),
        lax.psum_scatter(grad_proj_bias, "dp", scatter_dimension=0, tiled=True),
    )
    attn_shares = all_shares[:4]
    mlp_shares = all_shares[4:]
    return (
        mixed,
        input_grad,
        norm_shares[0],
        norm_shares[1],
        attn_shares[0],
        attn_shares[1],
        attn_shares[2],
        attn_shares[3],
        norm_shares[2],
        norm_shares[3],
        mlp_shares[0],
        mlp_shares[1],
        mlp_shares[2],
        mlp_shares[3],
    )


def solution(mesh):
    return jax.shard_map(
        shards,
        mesh=mesh,
        in_specs=(
            P(("dp", "tensor"), None),
            P(("dp", "tensor"), None),
            P("dp"),
            P("dp"),
            P("dp"),
            P("dp", None, "tensor"),
            P(None, "tensor", "dp"),
            P("tensor", "dp"),
            P("dp"),
            P("dp"),
            P("dp"),
            P("dp", "tensor"),
            P("tensor", "dp"),
            P("tensor", "dp"),
            P("dp"),
        ),
        out_specs=(
            P(("dp", "tensor"), None),
            P(("dp", "tensor"), None),
            P(("dp", "tensor")),
            P(("dp", "tensor")),
            P("dp", None, "tensor"),
            P(None, "tensor", "dp"),
            P("tensor", "dp"),
            P("dp"),
            P(("dp", "tensor")),
            P(("dp", "tensor")),
            P("dp", "tensor"),
            P("tensor", "dp"),
            P("tensor", "dp"),
            P("dp"),
        ),
        check_vma=False,
    )
```

profile of v0, /device:TPU:0, one launch (start us, length us, event | category | flops | bytes accessed | tf_op | source)
XLA Modules:
  0.0 1482.5 jit_solution(8059911205660535751)
XLA Ops:
  14.9 85.7 %all-reduce.9 = (bf16[1024]{0:T(1024)(128)(2,1)S(1)}, bf16[1024]{0:T(1024)(128)(2,1)S(1)}, bf16[1024]{0:T(1024)(128)(2,1)S(1)}, bf16[1024]{0:T(1024)(128)(2,1)S(1)}) all-reduce(bf16[1024]{0:T(1024)(128)(2,1)S(1)} %dynamic-update-slice, bf16[1024]{0:T(1024)(128)(2,1)S(1)} %dynamic-update-slice.1, ...), channel_id=1, replica_groups=mesh['dp'=32,'tensor'=4] {'dp'}, use_global_device_ids=true, to_apply=%add | all-reduce | flops 4096 | bytes 16384
  103.7 61.7 %all-gather.5.cloned.1.call-done = bf16[1024,769]{1,0:T(8,128)(2,1)} async-done(((bf16[32,769]{1,0:T(8,128)(2,1)}), bf16[1024,769]{1,0:T(8,128)(2,1)}) %all-gather.5.cloned.1.call-update) | async-done | bytes 1574928 | tf_op jit(solution)/shard_map/all_gather | solution.py:17
  169.5 4.7 all-to-all-start
  175.1 98.8 %all_gather.32 = bf16[2,4,64]{1,0,2:T(2,128)(2,1)S(1)} all-gather(bf16[2,4,2]{1,0,2:T(2,128)(2,1)S(1)} %copy.87), channel_id=1, replica_groups=mesh['dp'=32,'tensor'=4] {'dp'}, dimensions={2}, use_global_device_ids=true | all-gather | bytes 1056 | tf_op jit(solution)/shard_map/all_gather | solution.py:196
  274.3 86.9 %all_gather.33 = bf16[256,1024]{0,1:T(8,128)(2,1)} all-gather(bf16[256,32]{0,1:T(8,128)(2,1)S(1)} %copy-done.21), channel_id=1, replica_groups=mesh['dp'=32,'tensor'=4] {'dp'}, dimensions={1}, use_global_device_ids=true | all-gather | bytes 540672 | tf_op jit(solution)/shard_map/all_gather | solution.py:197
  361.1 1.9 copy.112
  363.0 3.9 add_convert_fusion
  367.0 19.7 %while.30 = (s32[]{:T(128)}, bf16[2,512,4,64]{1,3,2,0:T(8,128)(2,1)S(1)}, f32[2,4,512]{2,1,0:T(4,128)S(1)}, s32[2]{0:T(128)S(1)}, s32[1,1024]{1,0:T(1,128)S(1)},...) while((s32[]{:T(128)}, ...), condition=%wide.region_5.6_spmd, body=%wide.region_2.5_spmd.sunk | while | flops 563739136 | bytes 29964592 | solution.py:120
  370.2 1.7 fusion.126
  371.9 2.3 fusion.127
  374.2 2.5 fusion.128
  380.1 1.7 fusion.126
  381.8 2.3 fusion.127
  384.1 2.6 fusion.128
  388.9 3.9 fusion.74
  392.8 5.2 all-to-all-start.1
  399.8 68.0 %all-to-all-done.1 = f32[4,256,1024]{2,1,0:T(8,128)} async-done(((f32[4,256,1024]{2,1,0:T(8,128)}), f32[4,256,1024]{2,1,0:T(8,128)}, u32[]{:S(2)}, u32[]{:S(2)}) %all-to-all-start.1) | async-done | bytes 4194336 | tf_op jit(solution)/shard_map/all_to_all | solution.py:46
  467.8 3.7 reduce_sum.265
  473.8 41.8 %all_to_all.40 = bf16[4,256,1024]{2,1,0:T(8,128)(2,1)} all-to-all(bf16[4,256,1024]{2,1,0:T(8,128)(2,1)S(1)} %broadcast_in_dim.119), channel_id=1, replica_groups=mesh['dp'=32,'tensor'=4] {'tensor'}, dimensions={0} | all-to-all | bytes 4194304 | tf_op jit(solution)/shard_map/all_to_all | solution.py:24
  515.6 1.7 broadcast_in_dim.120
  517.3 4.9 all-to-all-start.4
  522.1 96.6 %all-gather = bf16[32,4,8]{2,1,0:T(4,128)(2,1)S(1)} all-gather(bf16[1,4,8]{2,1,0:T(4,128)(2,1)S(1)} %bitcast.256), channel_id=1, replica_groups=mesh['dp'=32,'tensor'=4] {'dp'}, dimensions={0}, use_global_device_ids=true | all-gather | bytes 2112 | tf_op jit(solution)/shard_map/all_gather | solution.py:203
  618.8 6.8 fusion.54
  625.6 8.9 convert_reduce_fusion.1
  634.6 4.4 fusion.52
  639.0 4.9 all-to-all-start.5
  643.9 7.6 fusion.80
  651.4 42.1 %all-to-all-done.5 = f32[4,256,1024]{2,1,0:T(8,128)} async-done(((f32[4,256,1024]{2,1,0:T(8,128)}), f32[4,256,1024]{2,1,0:T(8,128)}, u32[]{:S(2)}, u32[]{:S(2)}) %all-to-all-start.5) | async-done | bytes 4194336 | tf_op jit(solution)/shard_map/all_to_all | solution.py:46
  693.6 5.0 all-to-all-start.3
  698.6 3.4 fusion.82
  704.0 44.3 %all-to-all-done.3 = f32[4,256,1024]{2,1,0:T(8,128)} async-done(((f32[4,256,1024]{2,1,0:T(8,128)}), f32[4,256,1024]{2,1,0:T(8,128)}, u32[]{:S(2)}, u32[]{:S(2)}) %all-to-all-start.3) | async-done | bytes 4194336 | tf_op jit(solution)/shard_map/all_to_all | solution.py:46
  748.3 3.7 reduce_sum.268
  752.1 2.7 fusion.84
  757.6 4.5 all-to-all-start.6
  762.1 6.5 fusion.91
  768.6 20.7 %all-to-all-done.6 = bf16[4,256,1024]{2,1,0:T(8,128)(2,1)} async-done(((bf16[4,256,1024]{2,1,0:T(8,128)(2,1)}), bf16[4,256,1024]{2,1,0:T(8,128)(2,1)}, u32[]{:S(2)}, u32[]{:S(2)}) %all-to-all-start.6) | async-done | bytes 2097184 | tf_op jit(solution)/shard_map/all_to_all | solution.py:24
  789.3 2.0 convert_reduce_fusion.2
  791.3 5.2 pad_maximum_fusion
  796.4 5.6 copy.105
  803.7 3.6 fusion.90
  807.4 4.6 copy.86
  812.0 4.5 reshape.473
  816.5 7.5 fusion.79
  825.0 2.4 convolution_convert_fusion
  827.4 33.3 %while.31 = (s32[]{:T(128)}, bf16[2,512,4,64]{1,3,2,0:T(8,128)(2,1)S(1)}, f32[2,1024,4,64]{1,3,2,0:T(8,128)}, f32[2,1024,4,64]{1,3,2,0:T(8,128)}, s32[2]{0:T(128...) while((s32[]{:T(128)}, ...), condition=%wide.region_15.16_spmd, body=%wide.region_13.15_spmd.sunk | while | flops 1375730176 | bytes 104667600 | solution.py:163
  832.2 2.4 fusion.139
  834.7 3.2 multiply_reduce_fusion.5
  837.8 2.4 multiply_convert_fusion.5
  848.8 2.4 fusion.139
  851.2 3.2 multiply_reduce_fusion.5
  854.4 2.4 multiply_convert_fusion.5
  860.7 1.8 reduce_sum.273
  862.6 2.7 reduce_sum.272
  868.4 5.1 fusion.89
  873.5 2.4 dot_general.88
  875.9 6.4 fusion.56
  882.3 5.0 all-to-all-start.7
  889.3 2.0 convert_reduce_fusion
  891.7 225.0 %all-reduce.8 = (f32[2,4,64]{1,2,0:T(8,128)S(1)}, f32[8,128]{1,0:T(8,128)S(1)}, f32[1024]{0:T(1024)S(1)}) all-reduce(f32[2,4,64]{1,2,0:T(8,128)S(1)} %copy.96, f32[8,128]{1,0:T(8,128)S(1)} %bitcast.252, f32[1024]{0:T(1024)S(1)} %convert_reduce_fusion), channel_id=4, replica_groups=mesh['dp'=32,'tensor'=4] {'dp'}, use_global_device_ids=true, to_apply=%region_29.30.clone | all-reduce | flops 2560 | bytes 20480
  1118.7 2.9 fusion.81
  1122.5 64.7 %all-reduce.4 = f32[4,1024]{1,0:T(4,128)S(1)} all-reduce(f32[4,1024]{1,0:T(4,128)S(1)} %pad_maximum_fusion.4), channel_id=2, replica_groups=mesh['dp'=32,'tensor'=4] {'dp','tensor'}, use_global_device_ids=true, to_apply=%region_25.26.clone | all-reduce | flops 4096 | bytes 32768
  1190.6 1.7 slice.79
  1192.2 117.6 %reduce-scatter.14.cloned.1.call-done = f32[1024,32]{0,1:T(8,128)} async-done(((f32[1024,1024]{0,1:T(8,128)}), f32[1024,32]{0,1:T(8,128)}) %reduce-scatter.14.cloned.1.call-update) | async-done | bytes 131088 | tf_op jit(solution)/shard_map/reduce_scatter | solution.py:281
  1309.9 165.3 %reduce-scatter.10.cloned.1.call-done = f32[32,3,256]{2,0,1:T(8,128)} async-done(((f32[1024,3,256]{2,0,1:T(8,128)}), f32[32,3,256]{2,0,1:T(8,128)}) %reduce-scatter.10.cloned.1.call-update) | async-done | bytes 98320 | tf_op jit(solution)/shard_map/reduce_scatter | solution.py:276
  (203 shorter events, 54.6 us)
Async XLA Ops:
  7.2 158.1 %all-gather.5.cloned.1.call-start = ((), (), s32[]{:S(2)}) async-start(), calls=%async_computation.12 | async-start | bytes 1892352 | tf_op jit(solution)/shard_map/all_gather | solution.py:17
  100.6 65.8 %copy-start.14 = (f32[1024]{0:T(1024)}, f32[1024]{0:T(1024)S(1)}, u32[]{:S(2)}) copy-start(f32[1024]{0:T(1024)S(1)} %convert_element_type.171) | copy-start | bytes 12292
  101.8 64.6 %copy-start.17 = (f32[256]{0:T(256)}, f32[256]{0:T(256)S(1)}, u32[]{:S(2)}) copy-start(f32[256]{0:T(256)S(1)} %broadcast_multiply_fusion.1) | copy-start | bytes 3076
  103.1 0.5 copy-start.25
  103.7 62.8 %copy-start.22 = (f32[256]{0:T(256)}, f32[256]{0:T(256)S(1)}, u32[]{:S(2)}) copy-start(f32[256]{0:T(256)S(1)} %fusion.76) | copy-start | bytes 3076
  167.8 6.4 copy-start.30
  167.8 6.5 copy-start.16
  167.8 7.3 copy-start.29
  167.8 106.5 %copy-start.21 = (bf16[256,32]{0,1:T(8,128)(2,1)S(1)}, bf16[256,32]{0,1:T(8,128)(2,1)}, u32[]{:S(2)}) copy-start(bf16[256,32]{0,1:T(8,128)(2,1)} %param.26) | copy-start | bytes 49156
  169.5 191.6 %all-to-all-start = ((bf16[4,256,1024]{1,2,0:T(8,128)(2,1)}), bf16[4,256,1024]{1,2,0:T(8,128)(2,1)}, u32[]{:S(2)}, u32[]{:S(2)}) async-start(bf16[4,256,1024]{1,2,0:T(8,128)(2,1)} %broadcast_in_dim.117), calls=%async_computation | async-start | bytes 4194304 | tf_op jit(solution)/shard_map/all_to_all | solution.py:24
  174.2 224.5 %all-gather.7.cloned.1.call-start = ((), (), s32[]{:S(2)}) async-start(), calls=%async_computation.13 | async-start | bytes 2433024 | tf_op jit(solution)/shard_map/all_gather | solution.py:17
  363.0 4.0 copy-start.13
  386.7 6.1 copy-start.6
  392.8 75.0 %all-to-all-start.1 = ((f32[4,256,1024]{2,1,0:T(8,128)}), f32[4,256,1024]{2,1,0:T(8,128)}, u32[]{:S(2)}, u32[]{:S(2)}) async-start(f32[4,256,1024]{2,1,0:T(8,128)} %fusion.74), calls=%async_computation.1 | async-start | bytes 8388608 | tf_op jit(solution)/shard_map/all_to_all | solution.py:46
  397.9 73.6 %copy-start = (bf16[256,1024]{1,0:T(8,128)(2,1)S(1)}, bf16[256,1024]{1,0:T(8,128)(2,1)}, u32[]{:S(2)}) copy-start(bf16[256,1024]{1,0:T(8,128)(2,1)} %param.19) | copy-start | bytes 1572868
  397.9 227.7 %all-gather.9.cloned.1.call-start = ((), (), s32[]{:S(2)}) async-start(), calls=%async_computation.14 | async-start | bytes 2162688 | tf_op jit(solution)/shard_map/all_gather | solution.py:204
  473.2 42.3 %copy-start.5 = (bf16[256,1024]{1,0:T(8,128)(2,1)S(1)}, bf16[256,1024]{1,0:T(8,128)(2,1)}, u32[]{:S(2)}) copy-start(bf16[256,1024]{1,0:T(8,128)(2,1)} %param.20) | copy-start | bytes 1572868
  515.6 6.5 copy-start.28
  517.3 108.4 %all-to-all-start.4 = ((bf16[4,256,1024]{2,1,0:T(8,128)(2,1)}), bf16[4,256,1024]{2,1,0:T(8,128)(2,1)}, u32[]{:S(2)}, u32[]{:S(2)}) async-start(bf16[4,256,1024]{2,1,0:T(8,128)(2,1)} %broadcast_in_dim.120), calls=%async_computation.4 | async-start | bytes 4194304 | tf_op jit(solution)/shard_map/all_to_all | solution.py:24
  625.6 8.9 copy-start.19
  634.6 4.4 copy-start.31
  639.0 54.6 %all-to-all-start.5 = ((f32[4,256,1024]{2,1,0:T(8,128)}), f32[4,256,1024]{2,1,0:T(8,128)}, u32[]{:S(2)}, u32[]{:S(2)}) async-start(f32[4,256,1024]{2,1,0:T(8,128)} %bitcast.229), calls=%async_computation.5 | async-start | bytes 8388608 | tf_op jit(solution)/shard_map/all_to_all | solution.py:46
  693.6 54.7 %all-to-all-start.3 = ((f32[4,256,1024]{2,1,0:T(8,128)}), f32[4,256,1024]{2,1,0:T(8,128)}, u32[]{:S(2)}, u32[]{:S(2)}) async-start(f32[4,256,1024]{2,1,0:T(8,128)} %bitcast.228), calls=%async_computation.3 | async-start | bytes 8388608 | tf_op jit(solution)/shard_map/all_to_all | solution.py:46
  702.1 1.0 copy-start.4
  754.8 1.0 copy-start.2
  757.6 31.7 %all-to-all-start.6 = ((bf16[4,256,1024]{2,1,0:T(8,128)(2,1)}), bf16[4,256,1024]{2,1,0:T(8,128)(2,1)}, u32[]{:S(2)}, u32[]{:S(2)}) async-start(bf16[4,256,1024]{2,1,0:T(8,128)(2,1)} %broadcast_in_dim.123), calls=%async_computation.6 | async-start | bytes 4194304 | tf_op jit(solution)/shard_map/all_to_all | solution.py:24
  762.0 427.2 %reduce-scatter.16.cloned.1.call-start = ((), (), s32[]{:S(2)}) async-start(), calls=%async_computation.18 | async-start | bytes 4866048
  802.0 1.0 copy-start.7
  802.0 390.2 %reduce-scatter.12.cloned.1.call-start = ((), (), s32[]{:S(2)}) async-start(), calls=%async_computation.16 | async-start | bytes 1081344 | tf_op jit(solution)/shard_map/reduce_scatter | solution.py:278
  807.3 502.6 %reduce-scatter.14.cloned.1.call-start = ((), (), s32[]{:S(2)}) async-start(), calls=%async_computation.17 | async-start | bytes 4325376 | tf_op jit(solution)/shard_map/reduce_scatter | solution.py:281
  824.0 1.0 copy-start.8
  824.0 651.2 %reduce-scatter.10.cloned.1.call-start = ((), (), s32[]{:S(2)}) async-start(), calls=%async_computation.15 | async-start | bytes 3244032 | tf_op jit(solution)/shard_map/reduce_scatter | solution.py:276
  830.7 1.6 copy-start.9
  834.6 3.2 copy-start.10
  840.2 1.6 copy-start.11
  842.6 1.3 copy-start.12
  847.2 1.6 copy-start.9
  851.2 3.2 copy-start.10
  856.7 1.6 copy-start.11
  859.2 1.3 copy-start.12
  882.3 9.4 copy-start.27
  882.3 236.4 %all-to-all-start.7 = ((f32[4,256,1024]{2,1,0:T(8,128)}), f32[4,256,1024]{2,1,0:T(8,128)}, u32[]{:S(2)}, u32[]{:S(2)}) async-start(f32[4,256,1024]{2,1,0:T(8,128)} %fusion.56), calls=%async_computation.7 | async-start | bytes 8388608 | tf_op jit(solution)/shard_map/all_to_all | solution.py:46
  889.3 232.3 %copy-start.1 = (bf16[256,1024]{1,0:T(8,128)(2,1)S(1)}, bf16[256,1024]{1,0:T(8,128)(2,1)}, u32[]{:S(2)}) copy-start(bf16[256,1024]{1,0:T(8,128)(2,1)} %param.19) | copy-start | bytes 1572868
  889.3 232.3 %copy-start.15 = (f32[1024]{0:T(1024)S(1)}, f32[1024]{0:T(1024)}, u32[]{:S(2)}) copy-start(f32[1024]{0:T(1024)} %copy-done.14) | copy-start | bytes 12292
  889.3 232.3 %copy-start.18 = (f32[256]{0:T(256)S(1)}, f32[256]{0:T(256)}, u32[]{:S(2)}) copy-start(f32[256]{0:T(256)} %copy-done.17) | copy-start | bytes 3076
  891.3 230.6 %copy-start.26 = (f32[256]{0:T(256)S(1)}, f32[256]{0:T(256)}, u32[]{:S(2)}) copy-start(f32[256]{0:T(256)} %copy-done.25) | copy-start | bytes 3076
  891.3 230.6 %copy-start.23 = (f32[256]{0:T(256)S(1)}, f32[256]{0:T(256)}, u32[]{:S(2)}) copy-start(f32[256]{0:T(256)} %copy-done.22) | copy-start | bytes 3076
  1118.7 3.8 copy-start.20
  1118.7 3.8 copy-start.24
  1118.7 69.1 %copy-start.3 = (f32[256,1024]{1,0:T(8,128)S(1)}, f32[256,1024]{1,0:T(8,128)}, u32[]{:S(2)}) copy-start(f32[256,1024]{1,0:T(8,128)} %copy-done.2) | copy-start | bytes 3145732
Sparse Core Ops, SparseCore 0:
  10.2 155.0 all-gather.4
  177.2 156.1 all-gather.6
  400.4 151.5 all-gather.8
  802.2 177.1 reduce-scatter.15
  982.2 159.6 reduce-scatter.11
  1144.8 165.0 reduce-scatter.13
  1313.0 162.1 reduce-scatter.9
where the time goes:
time: 1490 us; the launch traced here: 1480 us
  blocking collectives  699 us (47%)
  waiting for transfers between devices  521 us (35%)
  matrix products  93.7 us (6%)
  other arithmetic  56.6 us (4%)
  local copies, waits for them, and re-layouts  51.5 us (3%)
  starting transfers between devices  34.5 us (2%)
  between operations  17.8 us (1%)
    unnamed x3, blocking collectives  375 us
    reduce_scatter x1, waiting for transfers between devices, shards(): lax.psum_scatter(grad_qkv, 'dp', scatter_dimension=0, tiled=True)  165 us
    all_to_all x4, waiting for transfers between devices, summed_on_arrival(): lax.all_to_all(cut_along(shard, dim, devices), axis, 0, 0, tiled=True)  154 us
    reduce_scatter x1, waiting for transfers between devices, shards(): lax.psum_scatter(grad_proj, 'dp', scatter_dimension=1, tiled=True)  118 us
    all_gather x1, blocking collectives, shards(): lax.all_gather(bias_qv, 'dp', axis=2, tiled=True)  98.8 us
    all_gather x1, blocking collectives, shards(): lax.all_gather(bias_fc, 'dp', axis=1, tiled=True)  96.6 us
    all_gather x1, blocking collectives, shards(): lax.all_gather(w_out, 'dp', axis=1, tiled=True)  86.9 us
    all_gather x2, waiting for transfers between devices, side_by_side(): out = lax.all_gather(both, axis, axis=dim, tiled=True)  61.7 us
  transfers between devices with their start and end apart: 14, of which 7 were waited for; matrix products, arithmetic and copies ran while one was open for 10% of the time, Pallas kernels for 0%

commit v1 on v0

v1 whole, which is shorter than its diff:
```python
import functools

import jax
import jax.numpy as jnp
from jax import lax
from jax.experimental import pallas as pl
from jax.experimental.pallas import tpu as pltpu
from jax.sharding import Mesh
from jax.sharding import PartitionSpec as P

HD = 64
SEQ = 1024
D = 1024
BLK = 256
HALF = 512
EPS = 1e-05
GELU_C = 0.7978845608028654
GELU_A = 0.044715
DP = ("x", "z", "yl")
TP = ("yh", "core")
ALL = DP + TP
SWAP = [(0, 1), (1, 0)]
f32 = jnp.float32
bf16 = jnp.bfloat16
VMEM_BYTES = 50 * 1024 * 1024


def kernel_call(body, grid, in_specs, out_specs, out_shape, flops, prefetch=0, scratch=()):
    return pl.pallas_call(
        body,
        out_shape=out_shape,
        grid_spec=pltpu.PrefetchScalarGridSpec(
            num_scalar_prefetch=prefetch,
            grid=grid,
            in_specs=in_specs,
            out_specs=out_specs,
            scratch_shapes=scratch,
        ),
        compiler_params=pltpu.CompilerParams(vmem_limit_bytes=VMEM_BYTES),
        cost_estimate=pl.CostEstimate(flops=flops, bytes_accessed=8 << 20, transcendentals=0),
    )


def shape(dims, dtype):
    return jax.ShapeDtypeStruct(dims, dtype)


def mm(a, b):
    return jnp.dot(a, b, preferred_element_type=f32)


def mm_nt(a, b):
    return lax.dot_general(a, b, (((1,), (1,)), ((), ())), preferred_element_type=f32)


def mm_tn(a, b):
    return lax.dot_general(a, b, (((0,), (0,)), ((), ())), preferred_element_type=f32)


def normalized(values):
    centered = values - jnp.mean(values, axis=-1, keepdims=True)
    variance = jnp.mean(centered * centered, axis=-1, keepdims=True)
    root = lax.rsqrt(variance + EPS)
    return centered * root, root


def norm_pull(grad, xhat, root, gain):
    scaled = grad * gain
    return root * (
        scaled
        - jnp.mean(scaled, axis=-1, keepdims=True)
        - xhat * jnp.mean(scaled * xhat, axis=-1, keepdims=True)
    )


def rows(width, move=lambda i: i, height=BLK):
    return pl.BlockSpec((height, width), lambda i, *_: (move(i), 0))


def whole(dims):
    return pl.BlockSpec(dims, lambda *_: (0,) * len(dims))


def qkv_body(x_ref, w_ref, small_ref, bias_ref, n_ref, j_ref):
    xhat, _ = normalized(x_ref[...].astype(f32))
    low = (xhat * small_ref[0:1, :] + small_ref[1:2, :]).astype(bf16)
    n_ref[...] = low
    j_ref[...] = (mm(low, w_ref[:, :768]) + bias_ref[...]).astype(bf16)


def qkv_rows(x_all, packed, smalls, bias_row):
    return kernel_call(
        qkv_body,
        (4,),
        [rows(D), whole((D, 896)), whole((8, D)), whole((1, 768))],
        [rows(D), rows(768)],
        [shape((SEQ, D), bf16), shape((SEQ, 768), bf16)],
        2 * SEQ * D * 768,
    )(x_all, packed, smalls, bias_row)


def allowed_block(segc_ref, segr_ref, s):
    width = (s + 1) * BLK
    same = segc_ref[s * BLK : width, :] == segr_ref[:, :width]
    row_at = lax.broadcasted_iota(jnp.int32, (BLK, width), 0) + s * BLK
    key_at = lax.broadcasted_iota(jnp.int32, (BLK, width), 1)
    return same & (key_at <= row_at)


def place(loc_ref, s):
    return pl.ds(pl.multiple_of(loc_ref[s] * BLK, BLK), BLK)


def softmax_rows(scores, mask):
    scores = jnp.where(mask, scores, -1e30)
    highest = jnp.max(scores, axis=-1, keepdims=True)
    expanded = jnp.exp(scores - highest)
    return expanded * (1.0 / jnp.sum(expanded, axis=-1, keepdims=True))


def attend_body(loc_ref, segc_ref, segr_ref, q_ref, k_ref, v_ref, o_ref, kn, vn):
    first = lax.broadcasted_iota(jnp.int32, (1, 128), 1) < HD
    for s in range(4):
        kn[s * BLK : (s + 1) * BLK, :] = k_ref[place(loc_ref, s), :]
        vn[s * BLK : (s + 1) * BLK, :] = v_ref[place(loc_ref, s), :]
    for s in range(4):
        width = (s + 1) * BLK
        mask = allowed_block(segc_ref, segr_ref, s)
        q = q_ref[place(loc_ref, s), :] * jnp.asarray(HD**-0.5, bf16)
        done = []
        for mine in (first, ~first):
            qh = jnp.where(mine, q, jnp.zeros_like(q))
            probs = softmax_rows(mm_nt(qh, kn[:width, :]), mask).astype(bf16)
            done.append(mm(probs, vn[:width, :]))
        o_ref[place(loc_ref, s), :] = jnp.where(first, done[0], done[1]).astype(bf16)


def column_block(at):
    return pl.BlockSpec((SEQ, 128), lambda p, *_: (0, at + p))


def attend_forward(loc, segc, segr, joined):
    return kernel_call(
        attend_body,
        (2,),
        [whole((SEQ, 1)), whole((1, SEQ)), column_block(0), column_block(2), column_block(4)],
        column_block(0),
        shape((SEQ, 256), bf16),
        4 * SEQ * SEQ * 256,
        prefetch=1,
        scratch=[pltpu.VMEM((SEQ, 128), bf16)] * 2,
    )(loc, segc, segr, joined, joined, joined)


def attend_back_body(
    loc_ref, segc_ref, segr_ref, q_ref, k_ref, v_ref, d_ref, dq_ref, dk_ref, dv_ref, kn, vn, dk, dv
):
    first = lax.broadcasted_iota(jnp.int32, (1, 128), 1) < HD
    for s in range(4):
        kn[s * BLK : (s + 1) * BLK, :] = k_ref[place(loc_ref, s), :]
        vn[s * BLK : (s + 1) * BLK, :] = v_ref[place(loc_ref, s), :]
    for s in (3, 2, 1, 0):
        width = (s + 1) * BLK
        mask = allowed_block(segc_ref, segr_ref, s)
        q = q_ref[place(loc_ref, s), :] * jnp.asarray(HD**-0.5, bf16)
        d = d_ref[place(loc_ref, s), :]
        keys = kn[:width, :]
        values = vn[:width, :]
        dq_sum, dk_sum, dv_sum = [], [], []
        for mine in (first, ~first):
            qh = jnp.where(mine, q, jnp.zeros_like(q))
            dh = jnp.where(mine, d, jnp.zeros_like(d))
            probs = softmax_rows(mm_nt(qh, keys), mask)
            d_probs = mm_nt(dh, values)
            d_scores = (
                probs * (d_probs - jnp.sum(probs * d_probs, axis=-1, keepdims=True))
            ).astype(bf16)
            dq_sum.append(mm(d_scores, keys))
            dk_sum.append(mm_tn(d_scores, qh))
            dv_sum.append(mm_tn(probs.astype(bf16), dh))
        dq = jnp.where(first, dq_sum[0], dq_sum[1]) * (HD**-0.5)
        dq_ref[place(loc_ref, s), :] = dq.astype(bf16)
        if s == 3:
            dk[...] = dk_sum[0] + dk_sum[1]
            dv[...] = dv_sum[0] + dv_sum[1]
        else:
            dk[:width, :] += dk_sum[0] + dk_sum[1]
            dv[:width, :] += dv_sum[0] + dv_sum[1]
    for s in range(4):
        dk_ref[place(loc_ref, s), :] = dk[s * BLK : (s + 1) * BLK, :].astype(bf16)
        dv_ref[place(loc_ref, s), :] = dv[s * BLK : (s + 1) * BLK, :].astype(bf16)


def attend_backward(loc, segc, segr, joined, d_context):
    return kernel_call(
        attend_back_body,
        (2,),
        [
            whole((SEQ, 1)),
            whole((1, SEQ)),
            column_block(0),
            column_block(2),
            column_block(4),
            column_block(0),
        ],
        [column_block(0)] * 3,
        [shape((SEQ, 256), bf16)] * 3,
        10 * SEQ * SEQ * 256,
        prefetch=1,
        scratch=[pltpu.VMEM((SEQ, 128), bf16)] * 2 + [pltpu.VMEM((SEQ, 128), f32)] * 2,
    )(loc, segc, segr, joined, joined, joined, d_context)


def out_other_body(c_ref, w_ref, o_ref):
    o_ref[...] = mm_nt(c_ref[...], w_ref[...]).astype(bf16)


OUT_COLUMNS = pl.BlockSpec((D, 256), lambda *_: (0, 8))
FC_COLUMNS = pl.BlockSpec((D, D), lambda *_: (0, 0))
PROJ_COLUMNS = pl.BlockSpec((D, D), lambda *_: (0, 1))


def out_other(context, packed):
    return kernel_call(
        out_other_body,
        (2,),
        [rows(256, lambda i: i + 2), OUT_COLUMNS],
        rows(D),
        shape((HALF, D), bf16),
        2 * HALF * D * 256,
    )(context, packed)


def out_mine_body(c_ref, w_ref, r_ref, s_ref, low_ref):
    total = mm_nt(c_ref[...], w_ref[...]) + r_ref[...].astype(f32)
    s_ref[...] = total
    low_ref[...] = total.astype(bf16)


def out_mine(context, packed, received):
    return kernel_call(
        out_mine_body,
        (2,),
        [rows(256), OUT_COLUMNS, rows(D)],
        [rows(D), rows(D)],
        [shape((HALF, D), f32), shape((HALF, D), bf16)],
        2 * HALF * D * 256,
    )(context, packed, received)


def middle_body(x_ref, s_ref, r_ref, small_ref, mid_ref, n_ref):
    middle = (
        x_ref[...].astype(f32) + (s_ref[...] + r_ref[...].astype(f32)) + small_ref[2:3, :]
    )
    mid_ref[...] = middle
    xhat, _ = normalized(middle)
    n_ref[...] = (xhat * small_ref[3:4, :] + small_ref[4:5, :]).astype(bf16)


def middle_rows(x_mine, s, r, smalls):
    return kernel_call(
        middle_body,
        (2,),
        [rows(D), rows(D), rows(D, lambda i: 1 - i), whole((8, D))],
        [rows(D), rows(D)],
        [shape((HALF, D), f32), shape((HALF, D), bf16)],
        HALF * D * 10,
    )(x_mine, s, r, smalls)


def feed_body(n_ref, g_ref, fc_ref, proj_ref, b_ref, a_ref, dh_ref, m_ref, dn_ref, sum_ref):
    hidden = mm(n_ref[...], fc_ref[...]) + b_ref[...]
    squared = hidden * hidden
    bent = jnp.tanh(GELU_C * (hidden + GELU_A * (squared * hidden)))
    half = 0.5 * (1.0 + bent)
    active = (hidden * half).astype(bf16)
    slope = half + (0.5 * hidden) * (1.0 - bent * bent) * (
        GELU_C + (3.0 * GELU_A * GELU_C) * squared
    )
    g = g_ref[...]
    d_hidden = (mm(g, proj_ref[...]) * slope).astype(bf16)
    a_ref[...] = active
    dh_ref[...] = d_hidden
    dn_ref[...] = mm_nt(d_hidden, fc_ref[...]).astype(dn_ref.dtype)
    m_ref[...] = mm_nt(active, proj_ref[...]).astype(m_ref.dtype)

    @pl.when(pl.program_id(0) == 0)
    def _():
        sum_ref[...] = jnp.zeros_like(sum_ref)

    sum_ref[0:1, :] += jnp.sum(d_hidden.astype(f32), axis=0, keepdims=True)


def feed_rows(normed, cot, packed, fc_bias, dtype):
    return kernel_call(
        feed_body,
        (2,),
        [rows(D), rows(D), FC_COLUMNS, PROJ_COLUMNS, whole((1, D))],
        [rows(D), rows(D), rows(D), rows(D), whole((8, D))],
        [
            shape((HALF, D), bf16),
            shape((HALF, D), bf16),
            shape((HALF, D), dtype),
            shape((HALF, D), dtype),
            shape((8, D), f32),
        ],
        8 * HALF * D * D,
    )(normed, cot, packed, packed, fc_bias)


def grad_pair_body(a0_ref, a1_ref, b0_ref, b1_ref, o_ref):
    total = mm_tn(a0_ref[...], b0_ref[...]) + mm_tn(a1_ref[...], b1_ref[...])
    o_ref[...] = total.astype(bf16)


def grad_pair(a0, a1, b0, b1):
    width = b0.shape[1]
    return kernel_call(
        grad_pair_body,
        (4,),
        [pl.BlockSpec((HALF, BLK), lambda i: (0, i))] * 2 + [whole((HALF, width))] * 2,
        rows(width),
        shape((D, width), bf16),
        2 * SEQ * D * width,
    )(a0, a1, b0, b1)


def mid_grad_body(s_ref, r_ref, mid_ref, g_ref, small_ref, dm_ref, low_ref, sum_ref):
    d_normed = s_ref[...] + r_ref[...].astype(f32)
    xhat, root = normalized(mid_ref[...])
    g = g_ref[...].astype(f32)
    d_middle = g + norm_pull(d_normed, xhat, root, small_ref[3:4, :])
    dm_ref[...] = d_middle
    low = d_middle.astype(bf16)
    low_ref[...] = low

    @pl.when(pl.program_id(0) == 0)
    def _():
        sum_ref[0:1, :] = jnp.sum(d_normed * xhat, axis=0, keepdims=True)
        sum_ref[1:2, :] = jnp.sum(d_normed, axis=0, keepdims=True)
        sum_ref[2:3, :] = jnp.sum(g, axis=0, keepdims=True)
        sum_ref[3:4, :] = jnp.sum(low.astype(f32), axis=0, keepdims=True)
        sum_ref[4:8, :] = jnp.zeros((4, D), f32)


def mid_grad(s, r, middle, cot_mine, smalls):
    return kernel_call(
        mid_grad_body,
        (2,),
        [rows(D), rows(D, lambda i: 1 - i), rows(D), rows(D), whole((8, D))],
        [rows(D), rows(D), whole((8, D))],
        [shape((HALF, D), f32), shape((HALF, D), bf16), shape((8, D), f32)],
        HALF * D * 20,
    )(s, r, middle, cot_mine, smalls)


def context_grad_body(d0_ref, d1_ref, w_ref, o_ref):
    o_ref[:HALF, :] = mm(d0_ref[...], w_ref[...]).astype(bf16)
    o_ref[HALF:, :] = mm(d1_ref[...], w_ref[...]).astype(bf16)


def context_grad(d0, d1, packed):
    return kernel_call(
        context_grad_body,
        (1,),
        [whole((HALF, D))] * 2 + [OUT_COLUMNS],
        whole((SEQ, 256)),
        shape((SEQ, 256), bf16),
        2 * SEQ * D * 256,
    )(d0, d1, packed)


def norm_one_body(x_ref, q_ref, k_ref, v_ref, w_ref, o_ref, sum_ref):
    partial = (
        mm_nt(q_ref[...], w_ref[:, :256])
        + mm_nt(k_ref[...], w_ref[:, 256:512])
        + mm_nt(v_ref[...], w_ref[:, 512:768])
    )
    xhat, _ = normalized(x_ref[...].astype(f32))
    o_ref[...] = partial.astype(bf16)

    @pl.when(pl.program_id(0) == 0)
    def _():
        sum_ref[...] = jnp.zeros_like(sum_ref)

    sum_ref[0:1, :] += jnp.sum(partial * xhat, axis=0, keepdims=True)
    sum_ref[1:2, :] += jnp.sum(partial, axis=0, keepdims=True)
    sum_ref[2:3, :256] += jnp.sum(q_ref[...].astype(f32), axis=0, keepdims=True)
    sum_ref[2:3, 256:512] += jnp.sum(v_ref[...].astype(f32), axis=0, keepdims=True)


def norm_one_rows(x_all, dq, dk, dv, packed):
    return kernel_call(
        norm_one_body,
        (4,),
        [rows(D), rows(256), rows(256), rows(256), whole((D, 896))],
        [rows(D), whole((8, D))],
        [shape((SEQ, D), bf16), shape((8, D), f32)],
        2 * SEQ * D * 768,
    )(x_all, dq, dk, dv, packed)


def qkv_grad_body(n_ref, q_ref, k_ref, v_ref, o_ref):
    n = n_ref[...]
    o_ref[:, :256] = mm_tn(n, q_ref[...]).astype(bf16)
    o_ref[:, 256:512] = mm_tn(n, k_ref[...]).astype(bf16)
    o_ref[:, 512:768] = mm_tn(n, v_ref[...]).astype(bf16)


def qkv_grad(normed, dq, dk, dv):
    return kernel_call(
        qkv_grad_body,
        (4,),
        [pl.BlockSpec((SEQ, BLK), lambda i: (0, i))] + [whole((SEQ, 256))] * 3,
        rows(768),
        shape((D, 768), bf16),
        2 * SEQ * D * 768,
    )(normed, dq, dk, dv)


def input_grad_body(x_ref, a_ref, b_ref, c_ref, d_ref, dm_ref, small_ref, o_ref):
    d_normed = (a_ref[...].astype(f32) + b_ref[...].astype(f32)) + (
        c_ref[...].astype(f32) + d_ref[...].astype(f32)
    )
    xhat, root = normalized(x_ref[...].astype(f32))
    o_ref[...] = dm_ref[...] + norm_pull(d_normed, xhat, root, small_ref[0:1, :])


def swap(values, axis):
    return lax.ppermute(values, axis, SWAP)


def to_owners(grad):
    parts = lax.all_to_all(grad.reshape(32, 32, grad.shape[1]), DP, 0, 0, tiled=True)
    return jnp.sum(parts.astype(f32), axis=0)


def shards(
    tokens,
    cotangent,
    segments,
    ln1_gain,
    ln1_bias,
    w_qkv,
    bias_qv,
    w_out,
    bias_out,
    ln2_gain,
    ln2_bias,
    w_fc,
    bias_fc,
    w_proj,
    bias_proj,
):
    yh, core, yl = lax.axis_index("yh"), lax.axis_index("core"), lax.axis_index("yl")
    tiny = jnp.stack(
        [
            ln1_gain,
            ln1_bias,
            bias_out,
            ln2_gain,
            ln2_bias,
            bias_proj,
            jnp.pad(bias_qv.reshape(16), (0, 16)),
            bias_fc.reshape(32),
        ],
        axis=1,
    )
    first_pack = jnp.concatenate(
        [w_qkv.reshape(32, 768), jnp.pad(tiny, ((0, 0), (0, 120)))], axis=1
    )
    packed_qkv = lax.all_to_all(
        jnp.broadcast_to(first_pack, (32, 32, 896)), DP, 0, 0, tiled=True
    ).reshape(D, 896)
    second_pack = jnp.concatenate([w_fc, w_proj.T, w_out.T], axis=1)
    neighbour = swap(second_pack, "yl")
    both = jnp.where(
        yl == 0,
        jnp.concatenate([second_pack, neighbour]),
        jnp.concatenate([neighbour, second_pack]),
    )
    packed = lax.all_gather(both, ("x", "z"), axis=0, tiled=True)

    x_mine = jnp.concatenate([tokens, swap(tokens, "yh")])
    x_all = jnp.concatenate([x_mine, swap(x_mine, "core")])
    cot_mine = jnp.concatenate([cotangent, swap(cotangent, "yh")])
    cot_other = swap(cot_mine, "core")

    small_t = packed_qkv[:, 768:776].T
    smalls = small_t.astype(f32)
    qv = small_t[6].reshape(32, 32)[:, :16].reshape(32, 2, 4, 2).transpose(1, 2, 0, 3)
    qv = qv.reshape(2, 256).astype(f32)
    bias_row = jnp.concatenate([qv[0], jnp.zeros((256,), f32), qv[1]])[None]
    fc_bias = small_t[7].reshape(32, 8, 4).transpose(1, 0, 2).reshape(1, D).astype(f32)

    at = jnp.arange(4, dtype=jnp.int32)
    loc = (at // 2 != yh).astype(jnp.int32) + 2 * (at % 2 != core).astype(jnp.int32)
    segc, segr = segments.reshape(SEQ, 1), segments.reshape(1, SEQ)

    normed_one, joined = qkv_rows(x_all, packed_qkv, smalls, bias_row)
    context = attend_forward(loc, segc, segr, joined)
    received = swap(out_other(context, packed), "core")
    s_out, s_out_low = out_mine(context, packed, received)
    middle, n2_mine = middle_rows(x_mine, s_out, swap(s_out_low, "yh"), smalls)
    n2_other = swap(n2_mine, "core")

    act0, dh0, mlp0, dn0, sum0 = feed_rows(n2_mine, cot_mine, packed, fc_bias, f32)
    act1, dh1, mlp1, dn1, sum1 = feed_rows(n2_other, cot_other, packed, fc_bias, bf16)
    s_dn = dn0 + swap(dn1, "core").astype(f32)
    r_dn = swap(s_dn.astype(bf16), "yh")
    s_mlp = mlp0 + swap(mlp1, "core").astype(f32)
    r_mlp = swap(s_mlp[BLK:].astype(bf16), "yh")
    mixed = (
        middle[:BLK] + (s_mlp[:BLK] + r_mlp.astype(f32)) + smalls[5:6]
    ).astype(bf16)
    grad_fc = to_owners(grad_pair(n2_mine, n2_other, dh0, dh1))
    grad_proj = to_owners(grad_pair(cot_mine, cot_other, act0, act1)).T

    d_middle, d_mid0, mid_sums = mid_grad(s_dn, r_dn, middle, cot_mine, smalls)
    d_mid1 = swap(d_mid0, "core")
    d_context = context_grad(d_mid0, d_mid1, packed)
    grad_out = to_owners(grad_pair(d_mid0, d_mid1, context[:HALF], context[HALF:])).T

    dq, dk, dv = attend_backward(loc, segc, segr, joined, d_context)
    grad_qkv = to_owners(qkv_grad(normed_one, dq, dk, dv)).reshape(32, 3, 256)
    d_n1, one_sums = norm_one_rows(x_all, dq, dk, dv, packed_qkv)
    from_core = swap(d_n1[HALF:], "core")
    s_n1 = d_n1[BLK:HALF].astype(f32) + from_core[BLK:].astype(f32)
    from_far = swap(s_n1.astype(bf16), "yh")
    input_grad = kernel_call(
        input_grad_body,
        (1,),
        [whole((BLK, D))] * 2
        + [whole((BLK, D))] * 4
        + [whole((8, D))],
        whole((BLK, D)),
        shape((BLK, D), f32),
        BLK * D * 20,
    )(
        tokens,
        d_n1[:BLK],
        from_core[:BLK],
        from_far,
        jnp.zeros_like(from_far),
        d_middle[:BLK],
        smalls,
    )

    mine = (jnp.arange(4) == 2 * yh + core).astype(f32)[None, :, None]
    norms = jnp.concatenate([one_sums[0:2], mid_sums[0:2]]).reshape(4, 32, 4, 8)
    biases = mid_sums[2:4].reshape(2, 32, 1, 32)
    fc_sum = (sum0[0] + sum1[0]).reshape(8, 32, 4).transpose(1, 0, 2).reshape(32, 1, 32)
    qv_sum = one_sums[2, :512].reshape(2, 4, 32, 2).transpose(2, 0, 1, 3).reshape(32, 1, 16)
    small_out = jnp.concatenate(
        [norms[0], norms[1], norms[2], norms[3]]
        + [jnp.broadcast_to(biases[k], (32, 4, 32)) for k in range(2)]
        + [fc_sum * mine, qv_sum * mine, jnp.zeros((32, 4, 112), f32)],
        axis=2,
    ).reshape(128, 1, 256)
    small_in = jnp.sum(lax.all_to_all(small_out, ALL, 0, 0, tiled=True), axis=(0, 1))
    return (
        mixed,
        input_grad,
        small_in[0:8],
        small_in[8:16],
        grad_qkv,
        small_in[128:144].reshape(2, 4, 2),
        grad_out,
        small_in[64:96],
        small_in[16:24],
        small_in[24:32],
        grad_fc,
        small_in[96:128].reshape(8, 4),
        grad_proj,
        small_in[32:64],
    )


def solution(mesh):
    fine = Mesh(mesh.devices.reshape(4, 4, 2, 2, 2), ALL)
    tok, dp, tp = P(ALL, None), DP, TP
    return jax.shard_map(
        shards,
        mesh=fine,
        in_specs=(
            tok,
            tok,
            P(dp),
            P(dp),
            P(dp),
            P(dp, None, tp),
            P(None, tp, dp),
            P(tp, dp),
            P(dp),
            P(dp),
            P(dp),
            P(dp, tp),
            P(tp, dp),
            P(tp, dp),
            P(dp),
        ),
        out_specs=(
            tok,
            tok,
            P(ALL),
            P(ALL),
            P(dp, None, tp),
            P(None, tp, dp),
            P(tp, dp),
            P(dp),
            P(ALL),
            P(ALL),
            P(dp, tp),
            P(tp, dp),
            P(tp, dp),
            P(dp),
        ),
        check_vma=False,
    )
```

time: 1490 us -> 365 us (0.24)
  blocking collectives: 699 us -> 0 us
  waiting for transfers between devices: 521 us -> 142 us
  matrix products: 93.7 us -> 0 us
  Pallas kernels: 0 us -> 87.4 us
  other arithmetic: 56.6 us -> 23.7 us
  starting transfers between devices: 34.5 us -> 59.1 us
  local copies, waits for them, and re-layouts: 51.5 us -> 34.8 us
    unnamed x3 -> x0, blocking collectives: 375 us -> none
    reduce_scatter x3 -> x0, waiting for transfers between devices: 283 us -> none  [the longest x1 165 us: shards(): lax.psum_scatter(grad_qkv, 'dp', scatter_dimension=0, tiled=True)]
    all_gather x3 -> x0, blocking collectives: 282 us -> none  [the longest x1 98.8 us: shards(): lax.all_gather(bias_qv, 'dp', axis=2, tiled=True)]
    all_to_all x7 -> x6, waiting for transfers between devices: 175 us -> 45 us  [the longest x4 25.1 us: to_owners(): lax.all_to_all(grad.reshape(32, 32, grad.shape[1]), DP, 0, 0, tiled=True)]
    dot_general x26 -> x0, matrix products: 93.7 us -> none  [the longest x4 22.7 us: inner_rows(): lax.dot_general(left_side, right_side, (((0,), (0,)), ((), ())), preferre...]
    pallas_call x0 -> x16, Pallas kernels: none -> 87.4 us  [the longest x2 17.2 us: feed_rows(): kernel_call(feed_body, (2,), [rows(D), rows(D), FC_COLUMNS, PROJ_COLUMNS,...]
    ppermute x0 -> x15, waiting for transfers between devices: none -> 83.1 us  [swap(): return lax.ppermute(values, axis, SWAP)]
    all_gather x3 -> x1, waiting for transfers between devices: 61.7 us -> 14.1 us  [shards(): packed = lax.all_gather(both, ('x', 'z'), axis=0, tiled=True)]
  transfers between devices with their start and end apart: 14 -> 22, of which waited for: 7 -> 13; matrix products, arithmetic and copies ran while one was open for 10% -> 13% of each run, Pallas kernels for 0% -> 20%
where the time goes in v1:
time: 365 us; the launch traced here: 362 us
  waiting for transfers between devices  142 us (39%)
  Pallas kernels  87.4 us (24%)
  starting transfers between devices  59.1 us (16%)
  local copies, waits for them, and re-layouts  34.8 us (10%)
  other arithmetic  23.7 us (6%)
  between operations  14.6 us (4%)
    ppermute x15, waiting for transfers between devices, swap(): return lax.ppermute(values, axis, SWAP)  83.1 us
    all_to_all x4, starting transfers between devices, to_owners(): lax.all_to_all(grad.reshape(32, 32, grad.shape[1]), DP, 0, 0, tiled=True)  26.6 us
    all_to_all x4, waiting for transfers between devices, to_owners(): lax.all_to_all(grad.reshape(32, 32, grad.shape[1]), DP, 0, 0, tiled=True)  25.1 us
    all_to_all x1, waiting for transfers between devices, shards(): lax.all_to_all(jnp.broadcast_to(first_pack, (32, 32, 896)), DP, 0, 0, til...  19.9 us
    pallas_call x2, Pallas kernels, feed_rows(): kernel_call(feed_body, (2,), [rows(D), rows(D), FC_COLUMNS, PROJ_COLUMNS,...  17.2 us
    ppermute x15, starting transfers between devices, swap(): return lax.ppermute(values, axis, SWAP)  16.6 us
    pallas_call x1, Pallas kernels, attend_backward(): kernel_call(attend_back_body, (2,), [whole((SEQ, 1)), whole((1, SEQ)), co...  14.8 us
    pallas_call x3, Pallas kernels, grad_pair(): kernel_call(grad_pair_body, (4,), [pl.BlockSpec((HALF, BLK), lambda i: (0...  14.1 us
  transfers between devices with their start and end apart: 22, of which 13 were waited for; matrix products, arithmetic and copies ran while one was open for 13% of the time, Pallas kernels for 20%

profile of v1, /device:TPU:0, one launch (start us, length us, event | category | flops | bytes accessed | tf_op | source)
XLA Modules:
  0.0 361.8 jit_solution(8266389117593455677)
XLA Ops:
  8.1 1.7 collective-permute-start.2
  9.9 3.8 %collective-permute-done.2 = bf16[32,2304]{1,0:T(8,128)(2,1)S(1)} collective-permute-done((bf16[32,2304]{1,0:T(8,128)(2,1)S(1)}, bf16[32,2304]{1,0:T(8,128)(2,1)S(1)}, u32[]{:S(2)}, u32[]{:S(2)}) %collective-permute-start.2) | collective-permute-done | bytes 147488 | tf_op jit(solution)/shard_map/ppermute | solution.py:430
  13.7 1.8 maximum_select_fusion
  15.5 3.4 collective-permute-start
  22.4 1.4 broadcast_in_dim.30
  23.8 8.4 %all-to-all-start = ((bf16[32,32,896]{2,1,0:T(8,128)(2,1)}), bf16[32,32,896]{2,1,0:T(8,128)(2,1)S(1)}, u32[]{:S(2)}, u32[]{:S(2)}) async-start(bf16[32,32,896]{2,1,0:T(8,128)(2,1)} %broadcast_in_dim.30), calls=%async_computation | async-start | bytes 3670016 | tf_op jit(solution)/shard_map/all_to_all | solution.py:472
  32.3 1.2 constant_dynamic-update-slice_fusion.3
  33.5 1.4 copy-done.29
  34.9 1.1 copy.129.segc_ref
  36.0 1.7 collective-permute-done.1
  37.7 2.3 constant_dynamic-update-slice_fusion.2.x_ref
  40.0 19.9 %all-to-all-done = bf16[32,32,896]{2,1,0:T(8,128)(2,1)S(1)} async-done(((bf16[32,32,896]{2,1,0:T(8,128)(2,1)}), bf16[32,32,896]{2,1,0:T(8,128)(2,1)S(1)}, u32[]{:S(2)}, u32[]{:S(2)}) %all-to-all-start) | async-done | bytes 1835040 | tf_op jit(solution)/shard_map/all_to_all | solution.py:472
  60.8 5.2 %shard_map.254 = (bf16[1024,1024]{1,0:T(8,128)(2,1)}, bf16[1024,768]{1,0:T(8,128)(2,1)S(1)}) custom-call(bf16[1024,1024]{1,0:T(8,128)(2,1)} %constant_dynamic-update-slice_fusion.2.x_ref, bf16[1024,896]{1,0:T(8,128)(2,1)S(1)} %bitcast.51, f32[8,1024]{1,0:T(8,128)S(1)} %bitcast_convert_fusion.small_ref, f32[1,768]{1,0:T(1,128)S(1)} %broadcast_in_dim.32.bias_ref), custom_call_target="tpu_custom_call" | custom-call | flops 1610612736 | bytes 8388608 | tf_op jit(solution)/shard_map/pallas_call | solution.py:92
  66.0 9.5 %shard_map.255.c_ref = bf16[1024,256]{1,0:T(8,128)(2,1)S(1)} custom-call(s32[4]{0:T(128)S(1)} %fusion.6.loc_ref, s32[1024,1]{1,0:T(8,128)S(1)} %copy-done.9, s32[1,1024]{1,0:T(1,128)S(1)} %bitcast.54, bf16[1024,768]{1,0:T(8,128)(2,1)S(1)} %get-tuple-element.38.q_ref.k_ref.v_ref, bf16[1024,768]{1,0:T(8,128)(2,1)S(1)} %get-tuple-element.38.q_ref.k_ref.v_ref, ...), custom_call_target="tpu_custom_call" | custom-call | flops 1073741824 | bytes 8388608 | tf_op jit(solution)/shard_map/pallas_call | solution.py:143
  75.4 14.1 %all-gather.2.cloned.1.call-done.w_ref.fc_ref.proj_ref = bf16[1024,2304]{1,0:T(8,128)(2,1)} async-done(((bf16[64,2304]{1,0:T(8,128)(2,1)}), bf16[1024,2304]{1,0:T(8,128)(2,1)}) %all-gather.2.cloned.1.call-update) | async-done | bytes 4718608 | tf_op jit(solution)/shard_map/all_gather | solution.py:482
  89.6 1.7 shard_map.256
  91.4 2.6 collective-permute-done.3.r_ref
  94.1 2.7 shard_map.257
  96.8 3.0 collective-permute-start.4
  100.3 34.4 %collective-permute-done.5 = bf16[256,1024]{1,0:T(8,128)(2,1)S(1)} collective-permute-done((bf16[256,1024]{1,0:T(8,128)(2,1)S(1)}, bf16[256,1024]{1,0:T(8,128)(2,1)S(1)}, u32[]{:S(2)}, u32[]{:S(2)}) %collective-permute-start.5) | collective-permute-done | bytes 524320 | tf_op jit(solution)/shard_map/ppermute | solution.py:430
  134.9 3.4 shard_map.258
  138.8 2.2 collective-permute-done.6.n_ref.a1_ref
  141.0 8.4 %shard_map.260 = (bf16[512,1024]{1,0:T(8,128)(2,1)S(1)}, bf16[512,1024]{1,0:T(8,128)(2,1)S(1)}, bf16[512,1024]{1,0:T(8,128)(2,1)S(1)}, bf16[512,1024]{1,0:T(8,128)(2,1)}, f32[8,1024]{1,0:T(8,128)S(1)}) custom-call(bf16[512,1024]{1,0:T(8,128)(2,1)} %collective-permute-done.6.n_ref.a1_ref, bf16[512,1024]{1,0:T(8,128)(2,1)} %collective-permute-done.7.g_ref.a1_ref, ...), custom_call_target="tpu_custom_call" | custom-call | flops 4294967296 | bytes 8388608 | tf_op jit(solution)/shard_map/pallas_call | solution.py:295
  149.4 1.0 copy-done.14
  150.4 1.0 copy-done.21
  151.5 1.0 copy-done.24
  152.7 8.8 %shard_map.259 = (bf16[512,1024]{1,0:T(8,128)(2,1)S(1)}, bf16[512,1024]{1,0:T(8,128)(2,1)S(1)}, f32[512,1024]{1,0:T(8,128)}, f32[512,1024]{1,0:T(8,128)}, f32[8,1024]{1,0:T(8,128)S(1)}) custom-call(bf16[512,1024]{1,0:T(8,128)(2,1)S(1)} %get-tuple-element.42.n_ref.a0_ref, bf16[512,1024]{1,0:T(8,128)(2,1)} %copy-done.5, ...), custom_call_target="tpu_custom_call" | custom-call | flops 4294967296 | bytes 8388608 | tf_op jit(solution)/shard_map/pallas_call | solution.py:295
  161.5 5.9 %shard_map.269 = bf16[1024,1024]{1,0:T(8,128)(2,1)} custom-call(bf16[512,1024]{1,0:T(8,128)(2,1)S(1)} %copy-done.6, bf16[512,1024]{1,0:T(8,128)(2,1)} %collective-permute-done.7.g_ref.a1_ref, bf16[512,1024]{1,0:T(8,128)(2,1)S(1)} %get-tuple-element.60.b0_ref, bf16[512,1024]{1,0:T(8,128)(2,1)} %copy-done.24), custom_call_target="tpu_custom_call" | custom-call | flops 2147483648 | bytes 8388608 | tf_op jit(solution)/shard_map/pallas_call | solution.py:318
  167.5 6.6 %all-to-all-start.5 = ((bf16[32,32,1024]{2,1,0:T(8,128)(2,1)}), bf16[32,32,1024]{2,1,0:T(8,128)(2,1)}, u32[]{:S(2)}, u32[]{:S(2)}) async-start(bf16[32,32,1024]{2,1,0:T(8,128)(2,1)} %bitcast.57), calls=%async_computation.5 | async-start | bytes 4194304 | tf_op jit(solution)/shard_map/all_to_all | solution.py:434
  174.1 4.2 %fusion.7 = (bf16[512,1024]{1,0:T(8,128)(2,1)}, f32[512,1024]{1,0:T(8,128)}) fusion(f32[512,1024]{1,0:T(8,128)} %get-tuple-element.45, bf16[512,1024]{1,0:T(8,128)(2,1)} %collective-permute-done.10), kind=kLoop, calls=%fused_computation.51 | loop fusion | flops 1572864 | bytes 6291456 | tf_op jit(solution)/shard_map/convert_element_type | solution.py:510
  178.3 2.7 collective-permute-start.11
  181.0 5.6 %shard_map.268 = bf16[1024,1024]{1,0:T(8,128)(2,1)} custom-call(bf16[512,1024]{1,0:T(8,128)(2,1)S(1)} %copy-done.16, bf16[512,1024]{1,0:T(8,128)(2,1)} %collective-permute-done.6.n_ref.a1_ref, bf16[512,1024]{1,0:T(8,128)(2,1)S(1)} %copy-done.23, bf16[512,1024]{1,0:T(8,128)(2,1)} %copy-done.21), custom_call_target="tpu_custom_call" | custom-call | flops 2147483648 | bytes 8388608 | tf_op jit(solution)/shard_map/pallas_call | solution.py:318
  186.6 16.2 %all-to-all-done.5 = bf16[32,32,1024]{2,1,0:T(8,128)(2,1)} async-done(((bf16[32,32,1024]{2,1,0:T(8,128)(2,1)}), bf16[32,32,1024]{2,1,0:T(8,128)(2,1)}, u32[]{:S(2)}, u32[]{:S(2)}) %all-to-all-start.5) | async-done | bytes 2097184 | tf_op jit(solution)/shard_map/all_to_all | solution.py:434
  202.8 6.5 %all-to-all-start.4 = ((bf16[32,32,1024]{2,1,0:T(8,128)(2,1)}), bf16[32,32,1024]{2,1,0:T(8,128)(2,1)}, u32[]{:S(2)}, u32[]{:S(2)}) async-start(bf16[32,32,1024]{2,1,0:T(8,128)(2,1)} %bitcast.56), calls=%async_computation.4 | async-start | bytes 4194304 | tf_op jit(solution)/shard_map/all_to_all | solution.py:434
  209.4 32.7 %collective-permute-done.11.r_ref = bf16[512,1024]{1,0:T(8,128)(2,1)S(1)} collective-permute-done((bf16[512,1024]{1,0:T(8,128)(2,1)}, bf16[512,1024]{1,0:T(8,128)(2,1)S(1)}, u32[]{:S(2)}, u32[]{:S(2)}) %collective-permute-start.11) | collective-permute-done | bytes 1048608 | tf_op jit(solution)/shard_map/ppermute | solution.py:430
  242.1 1.0 copy-done.11
  243.1 1.2 copy-done.12
  244.3 4.4 %shard_map.261 = (f32[512,1024]{1,0:T(8,128)}, bf16[512,1024]{1,0:T(8,128)(2,1)S(1)}, f32[8,1024]{1,0:T(8,128)S(1)}) custom-call(f32[512,1024]{1,0:T(8,128)} %get-tuple-element.139.s_ref, bf16[512,1024]{1,0:T(8,128)(2,1)S(1)} %copy-done.12, f32[512,1024]{1,0:T(8,128)} %get-tuple-element.41.mid_ref, bf16[512,1024]{1,0:T(8,128)(2,1)S(1)} %copy-done.6, ...), custom_call_target="tpu_custom_call" | custom-call | flops 10485760 | bytes 8388608 | tf_op jit(solution)/shard_map/pallas_call | solution.py:347
  251.4 1.7 shard_map.262.d_ref
  253.1 14.8 %shard_map.263 = (bf16[1024,256]{1,0:T(8,128)(2,1)S(1)}, bf16[1024,256]{1,0:T(8,128)(2,1)S(1)}, bf16[1024,256]{1,0:T(8,128)(2,1)S(1)}) custom-call(s32[4]{0:T(128)S(1)} %fusion.6.loc_ref, s32[1024,1]{1,0:T(8,128)S(1)} %copy-done.10, s32[1,1024]{1,0:T(1,128)S(1)} %bitcast.55, bf16[1024,768]{1,0:T(8,128)(2,1)} %copy-done, bf16[1024,768]{1,0:T(8,128)(2,1)} %copy-done, ...), custom_call_target="tpu_custom_call" | custom-call | flops 2684354560 | bytes 8388608 | tf_op jit(solution)/shard_map/pallas_call | solution.py:195
  268.0 5.8 %shard_map.264 = (bf16[1024,1024]{1,0:T(8,128)(2,1)}, f32[8,1024]{1,0:T(8,128)S(1)}) custom-call(bf16[1024,1024]{1,0:T(8,128)(2,1)} %constant_dynamic-update-slice_fusion.2.x_ref, bf16[1024,256]{1,0:T(8,128)(2,1)S(1)} %get-tuple-element.48.q_ref, bf16[1024,256]{1,0:T(8,128)(2,1)S(1)} %get-tuple-element.49.k_ref, ...), custom_call_target="tpu_custom_call" | custom-call | flops 1610612736 | bytes 8388608 | tf_op jit(solution)/shard_map/pallas_call | solution.py:393
  277.2 3.5 concatenate.56
  280.7 7.4 %all-to-all-start.1 = ((f32[128,1,256]{2,1,0:T(1,128)}), f32[128,1,256]{2,1,0:T(1,128)S(1)}, u32[]{:S(2)}, u32[]{:S(2)}) async-start(f32[128,1,256]{2,1,0:T(1,128)} %concatenate.56), calls=%async_computation.1 | async-start | bytes 262144 | tf_op jit(solution)/shard_map/all_to_all | solution.py:560
  288.1 2.2 convert_add_fusion.1
  290.2 1.3 copy-done.25
  292.4 2.5 collective-permute-start.9
  294.9 2.6 shard_map.267
  297.5 7.9 %all-to-all-start.3 = ((bf16[32,32,256]{2,1,0:T(8,128)(2,1)}), bf16[32,32,256]{2,1,0:T(8,128)(2,1)}, u32[]{:S(2)}, u32[]{:S(2)}) async-start(bf16[32,32,256]{2,1,0:T(8,128)(2,1)} %bitcast.31), calls=%async_computation.3 | async-start | bytes 1048576 | tf_op jit(solution)/shard_map/all_to_all | solution.py:434
  305.5 2.3 slice.154
  307.7 4.9 %shard_map.266 = bf16[1024,768]{1,0:T(8,128)(2,1)} custom-call(bf16[1024,1024]{1,0:T(8,128)(2,1)} %get-tuple-element.57.n_ref, bf16[1024,256]{1,0:T(8,128)(2,1)S(1)} %get-tuple-element.48.q_ref, bf16[1024,256]{1,0:T(8,128)(2,1)S(1)} %copy-done.18, bf16[1024,256]{1,0:T(8,128)(2,1)S(1)} %copy-done.20), custom_call_target="tpu_custom_call" | custom-call | flops 1610612736 | bytes 8388608 | tf_op jit(solution)/shard_map/pallas_call | solution.py:411
  312.6 4.9 %all-to-all-done.3 = bf16[32,32,256]{2,1,0:T(8,128)(2,1)} async-done(((bf16[32,32,256]{2,1,0:T(8,128)(2,1)}), bf16[32,32,256]{2,1,0:T(8,128)(2,1)}, u32[]{:S(2)}, u32[]{:S(2)}) %all-to-all-start.3) | async-done | bytes 524320 | tf_op jit(solution)/shard_map/all_to_all | solution.py:434
  317.5 5.6 %all-to-all-start.2 = ((bf16[32,32,768]{2,1,0:T(8,128)(2,1)}), bf16[32,32,768]{2,1,0:T(8,128)(2,1)}, u32[]{:S(2)}, u32[]{:S(2)}) async-start(bf16[32,32,768]{2,1,0:T(8,128)(2,1)} %bitcast.30), calls=%async_computation.2 | async-start | bytes 3145728 | tf_op jit(solution)/shard_map/all_to_all | solution.py:434
  323.1 2.5 fusion.2
  325.6 2.8 convert_reduce_fusion
  328.3 2.6 convert_reduce_fusion.1
  331.1 1.1 slice.153.a_ref
  334.4 2.2 add_convert_fusion
  336.6 1.3 collective-permute-start.14
  338.5 1.7 convert_reduce_fusion.3
  340.2 1.1 slice.187.b_ref
  341.3 4.0 %all-to-all-done.2 = bf16[32,32,768]{2,1,0:T(8,128)(2,1)} async-done(((bf16[32,32,768]{2,1,0:T(8,128)(2,1)}), bf16[32,32,768]{2,1,0:T(8,128)(2,1)}, u32[]{:S(2)}, u32[]{:S(2)}) %all-to-all-start.2) | async-done | bytes 1572896 | tf_op jit(solution)/shard_map/all_to_all | solution.py:434
  345.3 1.6 convert_reduce_fusion.2
  347.6 5.4 %collective-permute-done.14.c_ref = bf16[256,1024]{1,0:T(8,128)(2,1)S(1)} collective-permute-done((bf16[256,1024]{1,0:T(8,128)(2,1)}, bf16[256,1024]{1,0:T(8,128)(2,1)S(1)}, u32[]{:S(2)}, u32[]{:S(2)}) %collective-permute-start.14) | collective-permute-done | bytes 524320 | tf_op jit(solution)/shard_map/ppermute | solution.py:430
  353.1 1.9 shard_map.265
  (147 shorter events, 17.4 us)
Async XLA Ops:
  7.2 82.4 %all-gather.2.cloned.1.call-start = ((), (), s32[]{:S(2)}) async-start(), calls=%async_computation.6 | async-start | bytes 5013504 | tf_op jit(solution)/shard_map/all_gather | solution.py:482
  8.1 5.6 %collective-permute-start.2 = (bf16[32,2304]{1,0:T(8,128)(2,1)S(1)}, bf16[32,2304]{1,0:T(8,128)(2,1)S(1)}, u32[]{:S(2)}, u32[]{:S(2)}) collective-permute-start(bf16[32,2304]{1,0:T(8,128)(2,1)S(1)} %pad_maximum_fusion), channel_id=1, source_target_pairs={{0,4},{4,0},{1,5},{5,1},{2,6},{6,2},{3,7},{7,3},{8,12},{12,8},{9,1... | collective-permute-start | bytes 442376 | tf_op jit(solution)/shard_map/ppermute | solution.py:430
  15.5 16.8 %collective-permute-start = (bf16[256,1024]{1,0:T(8,128)(2,1)}, bf16[256,1024]{1,0:T(8,128)(2,1)}, u32[]{:S(2)}, u32[]{:S(2)}) collective-permute-start(bf16[256,1024]{1,0:T(8,128)(2,1)} %x_ref.1), channel_id=1, source_target_pairs={{0,2},{2,0},{1,3},{3,1},{4,6},{6,4},{5,7},{7,5},{8,10},{10,8},{9,1... | collective-permute-start | bytes 1572872 | tf_op jit(solution)/shard_map/ppermute | solution.py:430
  23.8 8.4 %copy-start.7 = (bf16[256,1024]{1,0:T(8,128)(2,1)S(1)}, bf16[256,1024]{1,0:T(8,128)(2,1)}, u32[]{:S(2)}) copy-start(bf16[256,1024]{1,0:T(8,128)(2,1)} %x_ref.1) | copy-start | bytes 1572868
  23.8 36.1 %all-to-all-start = ((bf16[32,32,896]{2,1,0:T(8,128)(2,1)}), bf16[32,32,896]{2,1,0:T(8,128)(2,1)S(1)}, u32[]{:S(2)}, u32[]{:S(2)}) async-start(bf16[32,32,896]{2,1,0:T(8,128)(2,1)} %broadcast_in_dim.30), calls=%async_computation | async-start | bytes 3670016 | tf_op jit(solution)/shard_map/all_to_all | solution.py:472
  32.2 2.7 copy-start.13
  33.5 1.4 copy-start.29
  34.9 25.9 %copy-start.3 = (bf16[512,1024]{1,0:T(8,128)(2,1)}, bf16[512,1024]{1,0:T(8,128)(2,1)S(1)}, u32[]{:S(2)}) copy-start(bf16[512,1024]{1,0:T(8,128)(2,1)S(1)} %get-tuple-element.143.x_ref) | copy-start | bytes 3145732
  34.9 2.8 collective-permute-start.1
  59.8 6.1 %copy-start.1 = (bf16[32,32,896]{2,1,0:T(8,128)(2,1)}, bf16[32,32,896]{2,1,0:T(8,128)(2,1)S(1)}, u32[]{:S(2)}) copy-start(bf16[32,32,896]{2,1,0:T(8,128)(2,1)S(1)} %all-to-all-done) | copy-start | bytes 5505028
  60.8 5.2 %copy-start.9 = (s32[1024,1]{1,0:T(8,128)S(1)}, s32[1024,1]{1,0:T(8,128)}, u32[]{:S(2)}) copy-start(s32[1024,1]{1,0:T(8,128)} %copy.129.segc_ref) | copy-start | bytes 12292
  65.9 9.5 %copy-start = (bf16[1024,768]{1,0:T(8,128)(2,1)}, bf16[1024,768]{1,0:T(8,128)(2,1)S(1)}, u32[]{:S(2)}) copy-start(bf16[1024,768]{1,0:T(8,128)(2,1)S(1)} %get-tuple-element.38.q_ref.k_ref.v_ref) | copy-start | bytes 4718596
  91.3 8.5 %copy-start.28 = (bf16[256,1024]{1,0:T(8,128)(2,1)S(1)}, bf16[256,1024]{1,0:T(8,128)(2,1)}, u32[]{:S(2)}) copy-start(bf16[256,1024]{1,0:T(8,128)(2,1)} %param.16) | copy-start | bytes 1572868
  91.3 2.7 collective-permute-start.3
  96.8 38.1 %copy-start.4 = (bf16[512,1024]{1,0:T(8,128)(2,1)S(1)}, bf16[512,1024]{1,0:T(8,128)(2,1)}, u32[]{:S(2)}) copy-start(bf16[512,1024]{1,0:T(8,128)(2,1)} %copy-done.3) | copy-start | bytes 3145732
  96.8 38.1 %collective-permute-start.4 = (bf16[512,1024]{1,0:T(8,128)(2,1)S(1)}, bf16[512,1024]{1,0:T(8,128)(2,1)S(1)}, u32[]{:S(2)}, u32[]{:S(2)}) collective-permute-start(bf16[512,1024]{1,0:T(8,128)(2,1)S(1)} %get-tuple-element.40), channel_id=1, source_target_pairs={{0,2},{2,0},{1,3},{3,1},{4,6},{6,4},{5,7},{7,5},{8,10},{10,8},{9,1... | collective-permute-start | bytes 3145736 | tf_op jit(solution)/shard_map/ppermute | solution.py:430
  99.8 34.9 %collective-permute-start.5 = (bf16[256,1024]{1,0:T(8,128)(2,1)S(1)}, bf16[256,1024]{1,0:T(8,128)(2,1)S(1)}, u32[]{:S(2)}, u32[]{:S(2)}) collective-permute-start(bf16[256,1024]{1,0:T(8,128)(2,1)S(1)} %copy-done.28), channel_id=1, source_target_pairs={{0,2},{2,0},{1,3},{3,1},{4,6},{6,4},{5,7},{7,5},{8,10},{10,8},{9,1... | collective-permute-start | bytes 1572872 | tf_op jit(solution)/shard_map/ppermute | solution.py:430
  134.7 3.5 copy-start.5
  134.7 4.1 %collective-permute-start.7 = (bf16[512,1024]{1,0:T(8,128)(2,1)S(1)}, bf16[512,1024]{1,0:T(8,128)(2,1)}, u32[]{:S(2)}, u32[]{:S(2)}) collective-permute-start(bf16[512,1024]{1,0:T(8,128)(2,1)S(1)} %constant_dynamic-update-slice_fusion.5.g_ref.a0_ref), channel_id=1, source_target_pairs={{0,1},{1,0},{2,3},{3,2},{4,5},{5,4},{6,7},{7,6},{8,9},{9,8},{10,11... | collective-permute-start | bytes 3145736 | tf_op jit(solution)/shard_map/ppermute | solution.py:430
  138.3 14.4 %copy-start.15 = (bf16[512,1024]{1,0:T(8,128)(2,1)}, bf16[512,1024]{1,0:T(8,128)(2,1)S(1)}, u32[]{:S(2)}) copy-start(bf16[512,1024]{1,0:T(8,128)(2,1)S(1)} %get-tuple-element.42.n_ref.a0_ref) | copy-start | bytes 3145732
  138.3 2.8 collective-permute-start.6
  149.4 1.0 copy-start.14
  150.4 1.0 copy-start.21
  151.5 1.0 copy-start.24
  152.4 9.1 %copy-start.6 = (bf16[512,1024]{1,0:T(8,128)(2,1)S(1)}, bf16[512,1024]{1,0:T(8,128)(2,1)}, u32[]{:S(2)}) copy-start(bf16[512,1024]{1,0:T(8,128)(2,1)} %copy-done.5) | copy-start | bytes 3145732
  152.4 21.6 %collective-permute-start.10 = (bf16[512,1024]{1,0:T(8,128)(2,1)}, bf16[512,1024]{1,0:T(8,128)(2,1)}, u32[]{:S(2)}, u32[]{:S(2)}) collective-permute-start(bf16[512,1024]{1,0:T(8,128)(2,1)} %get-tuple-element.46), channel_id=1, source_target_pairs={{0,1},{1,0},{2,3},{3,2},{4,5},{5,4},{6,7},{7,6},{8,9},{9,8},{10,11... | collective-permute-start | bytes 3145736 | tf_op jit(solution)/shard_map/ppermute | solution.py:430
  161.5 6.0 %copy-start.22 = (bf16[512,1024]{1,0:T(8,128)(2,1)}, bf16[512,1024]{1,0:T(8,128)(2,1)S(1)}, u32[]{:S(2)}) copy-start(bf16[512,1024]{1,0:T(8,128)(2,1)S(1)} %get-tuple-element.58.b0_ref) | copy-start | bytes 3145732
  167.5 35.4 %all-to-all-start.5 = ((bf16[32,32,1024]{2,1,0:T(8,128)(2,1)}), bf16[32,32,1024]{2,1,0:T(8,128)(2,1)}, u32[]{:S(2)}, u32[]{:S(2)}) async-start(bf16[32,32,1024]{2,1,0:T(8,128)(2,1)} %bitcast.57), calls=%async_computation.5 | async-start | bytes 4194304 | tf_op jit(solution)/shard_map/all_to_all | solution.py:434
  174.1 6.9 %copy-start.16 = (bf16[512,1024]{1,0:T(8,128)(2,1)S(1)}, bf16[512,1024]{1,0:T(8,128)(2,1)}, u32[]{:S(2)}) copy-start(bf16[512,1024]{1,0:T(8,128)(2,1)} %copy-done.15) | copy-start | bytes 3145732
  174.1 6.9 %copy-start.23 = (bf16[512,1024]{1,0:T(8,128)(2,1)S(1)}, bf16[512,1024]{1,0:T(8,128)(2,1)}, u32[]{:S(2)}) copy-start(bf16[512,1024]{1,0:T(8,128)(2,1)} %copy-done.22) | copy-start | bytes 3145732
  178.3 63.8 %collective-permute-start.11 = (bf16[512,1024]{1,0:T(8,128)(2,1)}, bf16[512,1024]{1,0:T(8,128)(2,1)S(1)}, u32[]{:S(2)}, u32[]{:S(2)}) collective-permute-start(bf16[512,1024]{1,0:T(8,128)(2,1)} %get-tuple-element.138), channel_id=1, source_target_pairs={{0,2},{2,0},{1,3},{3,1},{4,6},{6,4},{5,7},{7,5},{8,10},{10,8},{9,1... | collective-permute-start | bytes 3145736 | tf_op jit(solution)/shard_map/ppermute | solution.py:430
  202.8 77.8 %all-to-all-start.4 = ((bf16[32,32,1024]{2,1,0:T(8,128)(2,1)}), bf16[32,32,1024]{2,1,0:T(8,128)(2,1)}, u32[]{:S(2)}, u32[]{:S(2)}) async-start(bf16[32,32,1024]{2,1,0:T(8,128)(2,1)} %bitcast.56), calls=%async_computation.4 | async-start | bytes 4194304 | tf_op jit(solution)/shard_map/all_to_all | solution.py:434
  242.1 1.0 copy-start.11
  243.1 1.2 copy-start.12
  248.7 2.7 collective-permute-start.12
  249.2 38.8 %collective-permute-start.8 = (bf16[512,1024]{1,0:T(8,128)(2,1)}, bf16[512,1024]{1,0:T(8,128)(2,1)}, u32[]{:S(2)}, u32[]{:S(2)}) collective-permute-start(bf16[512,1024]{1,0:T(8,128)(2,1)} %copy-done.14), channel_id=1, source_target_pairs={{0,1},{1,0},{2,3},{3,2},{4,5},{5,4},{6,7},{7,6},{8,9},{9,8},{10,11... | collective-permute-start | bytes 3145736 | tf_op jit(solution)/shard_map/ppermute | solution.py:430
  251.2 1.9 copy-start.10
  253.1 14.9 %copy-start.2 = (bf16[32,32,896]{2,1,0:T(8,128)(2,1)S(1)}, bf16[32,32,896]{2,1,0:T(8,128)(2,1)}, u32[]{:S(2)}) copy-start(bf16[32,32,896]{2,1,0:T(8,128)(2,1)} %copy-done.1) | copy-start | bytes 5505028
  268.0 5.8 %copy-start.17 = (bf16[1024,256]{1,0:T(8,128)(2,1)}, bf16[1024,256]{1,0:T(8,128)(2,1)S(1)}, u32[]{:S(2)}) copy-start(bf16[1024,256]{1,0:T(8,128)(2,1)S(1)} %get-tuple-element.49.k_ref) | copy-start | bytes 1572868
  268.0 5.8 %copy-start.19 = (bf16[1024,256]{1,0:T(8,128)(2,1)}, bf16[1024,256]{1,0:T(8,128)(2,1)S(1)}, u32[]{:S(2)}) copy-start(bf16[1024,256]{1,0:T(8,128)(2,1)S(1)} %get-tuple-element.50.v_ref) | copy-start | bytes 1572868
  280.7 16.9 %all-to-all-start.1 = ((f32[128,1,256]{2,1,0:T(1,128)}), f32[128,1,256]{2,1,0:T(1,128)S(1)}, u32[]{:S(2)}, u32[]{:S(2)}) async-start(f32[128,1,256]{2,1,0:T(1,128)} %concatenate.56), calls=%async_computation.1 | async-start | bytes 262144 | tf_op jit(solution)/shard_map/all_to_all | solution.py:560
  290.2 1.3 copy-start.25
  292.4 30.7 %collective-permute-start.9 = (bf16[256,1024]{1,0:T(8,128)(2,1)}, bf16[256,1024]{1,0:T(8,128)(2,1)}, u32[]{:S(2)}, u32[]{:S(2)}) collective-permute-start(bf16[256,1024]{1,0:T(8,128)(2,1)} %slice.216), channel_id=1, source_target_pairs={{0,2},{2,0},{1,3},{3,1},{4,6},{6,4},{5,7},{7,5},{8,10},{10,8},{9,1... | collective-permute-start | bytes 1572872 | tf_op jit(solution)/shard_map/ppermute | solution.py:430
  297.5 10.2 %copy-start.18 = (bf16[1024,256]{1,0:T(8,128)(2,1)S(1)}, bf16[1024,256]{1,0:T(8,128)(2,1)}, u32[]{:S(2)}) copy-start(bf16[1024,256]{1,0:T(8,128)(2,1)} %copy-done.17) | copy-start | bytes 1572868
  297.5 10.2 %copy-start.20 = (bf16[1024,256]{1,0:T(8,128)(2,1)S(1)}, bf16[1024,256]{1,0:T(8,128)(2,1)}, u32[]{:S(2)}) copy-start(bf16[1024,256]{1,0:T(8,128)(2,1)} %copy-done.19) | copy-start | bytes 1572868
  297.5 20.0 %all-to-all-start.3 = ((bf16[32,32,256]{2,1,0:T(8,128)(2,1)}), bf16[32,32,256]{2,1,0:T(8,128)(2,1)}, u32[]{:S(2)}, u32[]{:S(2)}) async-start(bf16[32,32,256]{2,1,0:T(8,128)(2,1)} %bitcast.31), calls=%async_computation.3 | async-start | bytes 1048576 | tf_op jit(solution)/shard_map/all_to_all | solution.py:434
  307.7 26.7 %collective-permute-start.13 = (bf16[512,1024]{1,0:T(8,128)(2,1)}, bf16[512,1024]{1,0:T(8,128)(2,1)}, u32[]{:S(2)}, u32[]{:S(2)}) collective-permute-start(bf16[512,1024]{1,0:T(8,128)(2,1)} %slice.154), channel_id=1, source_target_pairs={{0,1},{1,0},{2,3},{3,2},{4,5},{5,4},{6,7},{7,6},{8,9},{9,8},{10,11... | collective-permute-start | bytes 3145736 | tf_op jit(solution)/shard_map/ppermute | solution.py:430
  312.6 10.5 %copy-start.26 = (f32[512,1024]{1,0:T(8,128)S(1)}, f32[512,1024]{1,0:T(8,128)}, u32[]{:S(2)}) copy-start(f32[512,1024]{1,0:T(8,128)} %copy-done.25) | copy-start | bytes 6291460
  317.5 27.8 %all-to-all-start.2 = ((bf16[32,32,768]{2,1,0:T(8,128)(2,1)}), bf16[32,32,768]{2,1,0:T(8,128)(2,1)}, u32[]{:S(2)}, u32[]{:S(2)}) async-start(bf16[32,32,768]{2,1,0:T(8,128)(2,1)} %bitcast.30), calls=%async_computation.2 | async-start | bytes 3145728 | tf_op jit(solution)/shard_map/all_to_all | solution.py:434
  325.6 5.4 %copy-start.27 = (f32[512,1024]{1,0:T(8,128)S(1)}, f32[512,1024]{1,0:T(8,128)}, u32[]{:S(2)}) copy-start(f32[512,1024]{1,0:T(8,128)} %get-tuple-element.52) | copy-start | bytes 6291460
  336.6 16.5 %copy-start.8 = (bf16[256,1024]{1,0:T(8,128)(2,1)S(1)}, bf16[256,1024]{1,0:T(8,128)(2,1)}, u32[]{:S(2)}) copy-start(bf16[256,1024]{1,0:T(8,128)(2,1)} %x_ref.1) | copy-start | bytes 1572868
  336.6 16.5 %collective-permute-start.14 = (bf16[256,1024]{1,0:T(8,128)(2,1)}, bf16[256,1024]{1,0:T(8,128)(2,1)S(1)}, u32[]{:S(2)}, u32[]{:S(2)}) collective-permute-start(bf16[256,1024]{1,0:T(8,128)(2,1)} %add_convert_fusion), channel_id=1, source_target_pairs={{0,2},{2,0},{1,3},{3,1},{4,6},{6,4},{5,7},{7,5},{8,10},{10,8},{9,1... | collective-permute-start | bytes 1572872 | tf_op jit(solution)/shard_map/ppermute | solution.py:430
Sparse Core Ops, SparseCore 0:
  15.6 73.8 all-gather.1

commit v2 on v1

--- a/solution.py
+++ b/solution.py
@@ -18,11 +18,12 @@
 GELU_A = 0.044715
 DP = ("x", "z", "yl")
 TP = ("yh", "core")
+XZ = ("x", "z")
 ALL = DP + TP
 SWAP = [(0, 1), (1, 0)]
 f32 = jnp.float32
 bf16 = jnp.bfloat16
-VMEM_BYTES = 50 * 1024 * 1024
+VMEM_BYTES = 60 * 1024 * 1024
 
 
 def kernel_call(body, grid, in_specs, out_specs, out_shape, flops, prefetch=0, scratch=()):
@@ -84,15 +85,15 @@
 def qkv_body(x_ref, w_ref, small_ref, bias_ref, n_ref, j_ref):
     xhat, _ = normalized(x_ref[...].astype(f32))
     low = (xhat * small_ref[0:1, :] + small_ref[1:2, :]).astype(bf16)
-    n_ref[...] = low
-    j_ref[...] = (mm(low, w_ref[:, :768]) + bias_ref[...]).astype(bf16)
+    n_ref[...] = xhat.astype(bf16)
+    j_ref[...] = (mm(low, w_ref[...]) + bias_ref[...]).astype(bf16)
 
 
 def qkv_rows(x_all, packed, smalls, bias_row):
     return kernel_call(
         qkv_body,
         (4,),
-        [rows(D), whole((D, 896)), whole((8, D)), whole((1, 768))],
+        [rows(D), whole((D, 768)), whole((8, D)), whole((1, 768))],
         [rows(D), rows(768)],
         [shape((SEQ, D), bf16), shape((SEQ, 768), bf16)],
         2 * SEQ * D * 768,
@@ -215,7 +216,7 @@
     o_ref[...] = mm_nt(c_ref[...], w_ref[...]).astype(bf16)
 
 
-OUT_COLUMNS = pl.BlockSpec((D, 256), lambda *_: (0, 8))
+OUT_COLUMNS = pl.BlockSpec((D, 256), lambda *_: (0, 3))
 FC_COLUMNS = pl.BlockSpec((D, D), lambda *_: (0, 0))
 PROJ_COLUMNS = pl.BlockSpec((D, D), lambda *_: (0, 1))
 
@@ -231,10 +232,20 @@
     )(context, packed)
 
 
-def out_mine_body(c_ref, w_ref, r_ref, s_ref, low_ref):
+def parted(here_ref, there_ref, values):
+    @pl.when(pl.program_id(0) == 0)
+    def _():
+        here_ref[...] = values
+
+    @pl.when(pl.program_id(0) == 1)
+    def _():
+        there_ref[...] = values
+
+
+def out_mine_body(c_ref, w_ref, r_ref, s_ref, here_ref, there_ref):
     total = mm_nt(c_ref[...], w_ref[...]) + r_ref[...].astype(f32)
     s_ref[...] = total
-    low_ref[...] = total.astype(bf16)
+    parted(here_ref, there_ref, total.astype(bf16))
 
 
 def out_mine(context, packed, received):
@@ -242,91 +253,133 @@
         out_mine_body,
         (2,),
         [rows(256), OUT_COLUMNS, rows(D)],
-        [rows(D), rows(D)],
-        [shape((HALF, D), f32), shape((HALF, D), bf16)],
+        [rows(D)] + [whole((BLK, D))] * 2,
+        [shape((HALF, D), f32)] + [shape((BLK, D), bf16)] * 2,
         2 * HALF * D * 256,
     )(context, packed, received)
 
 
-def middle_body(x_ref, s_ref, r_ref, small_ref, mid_ref, n_ref):
-    middle = (
-        x_ref[...].astype(f32) + (s_ref[...] + r_ref[...].astype(f32)) + small_ref[2:3, :]
-    )
+def arrived(here_ref, there_ref):
+    return jnp.where(pl.program_id(0) == 0, here_ref[...], there_ref[...]).astype(f32)
+
+
+def middle_body(x_ref, s_ref, here_ref, there_ref, small_ref, mid_ref, n_ref):
+    total = s_ref[...] + arrived(here_ref, there_ref)
+    middle = x_ref[...].astype(f32) + total + small_ref[2:3, :]
     mid_ref[...] = middle
     xhat, _ = normalized(middle)
     n_ref[...] = (xhat * small_ref[3:4, :] + small_ref[4:5, :]).astype(bf16)
 
 
-def middle_rows(x_mine, s, r, smalls):
+def middle_rows(x_mine, s, here, there, smalls):
     return kernel_call(
         middle_body,
         (2,),
-        [rows(D), rows(D), rows(D, lambda i: 1 - i), whole((8, D))],
+        [rows(D), rows(D)] + [whole((BLK, D))] * 2 + [whole((8, D))],
         [rows(D), rows(D)],
         [shape((HALF, D), f32), shape((HALF, D), bf16)],
         HALF * D * 10,
-    )(x_mine, s, r, smalls)
-
-
-def feed_body(n_ref, g_ref, fc_ref, proj_ref, b_ref, a_ref, dh_ref, m_ref, dn_ref, sum_ref):
-    hidden = mm(n_ref[...], fc_ref[...]) + b_ref[...]
-    squared = hidden * hidden
-    bent = jnp.tanh(GELU_C * (hidden + GELU_A * (squared * hidden)))
-    half = 0.5 * (1.0 + bent)
-    active = (hidden * half).astype(bf16)
-    slope = half + (0.5 * hidden) * (1.0 - bent * bent) * (
-        GELU_C + (3.0 * GELU_A * GELU_C) * squared
-    )
-    g = g_ref[...]
-    d_hidden = (mm(g, proj_ref[...]) * slope).astype(bf16)
-    a_ref[...] = active
-    dh_ref[...] = d_hidden
-    dn_ref[...] = mm_nt(d_hidden, fc_ref[...]).astype(dn_ref.dtype)
-    m_ref[...] = mm_nt(active, proj_ref[...]).astype(m_ref.dtype)
-
+    )(x_mine, s, here, there, smalls)
+
+
+def feed_core(n_ref, g_ref, fc_ref, proj_ref, b_ref, a_ref, dh_ref, sum_ref):
     @pl.when(pl.program_id(0) == 0)
     def _():
         sum_ref[...] = jnp.zeros_like(sum_ref)
 
-    sum_ref[0:1, :] += jnp.sum(d_hidden.astype(f32), axis=0, keepdims=True)
-
-
-def feed_rows(normed, cot, packed, fc_bias, dtype):
-    return kernel_call(
-        feed_body,
+    for at in range(0, D, BLK):
+        cut = slice(at, at + BLK)
+        hidden = mm(n_ref[...], fc_ref[:, cut]) + b_ref[:, cut]
+        d_active = mm(g_ref[...], proj_ref[:, cut])
+        squared = hidden * hidden
+        bent = jnp.tanh(hidden * (GELU_C + (GELU_A * GELU_C) * squared))
+        half = 0.5 + 0.5 * bent
+        slope = half + (0.5 * hidden) * (1.0 - bent * bent) * (
+            GELU_C + (3.0 * GELU_A * GELU_C) * squared
+        )
+        d_hidden = (d_active * slope).astype(bf16)
+        a_ref[:, cut] = (hidden * half).astype(bf16)
+        dh_ref[:, cut] = d_hidden
+        sum_ref[0:1, cut] += jnp.sum(d_hidden.astype(f32), axis=0, keepdims=True)
+
+
+def feed_other_body(
+    n_ref, g_ref, fc_ref, proj_ref, b_ref, a_ref, dh_ref, m_ref, dn_ref, sum_ref
+):
+    feed_core(n_ref, g_ref, fc_ref, proj_ref, b_ref, a_ref, dh_ref, sum_ref)
+    dn_ref[...] = mm_nt(dh_ref[...], fc_ref[...]).astype(bf16)
+    m_ref[...] = mm_nt(a_ref[...], proj_ref[...]).astype(bf16)
+
+
+def feed_other(normed, cot, packed, fc_bias):
+    return kernel_call(
+        feed_other_body,
         (2,),
         [rows(D), rows(D), FC_COLUMNS, PROJ_COLUMNS, whole((1, D))],
-        [rows(D), rows(D), rows(D), rows(D), whole((8, D))],
-        [
-            shape((HALF, D), bf16),
-            shape((HALF, D), bf16),
-            shape((HALF, D), dtype),
-            shape((HALF, D), dtype),
-            shape((8, D), f32),
-        ],
+        [rows(D)] * 4 + [whole((8, D))],
+        [shape((HALF, D), bf16)] * 4 + [shape((8, D), f32)],
         8 * HALF * D * D,
     )(normed, cot, packed, packed, fc_bias)
 
 
-def grad_pair_body(a0_ref, a1_ref, b0_ref, b1_ref, o_ref):
-    total = mm_tn(a0_ref[...], b0_ref[...]) + mm_tn(a1_ref[...], b1_ref[...])
-    o_ref[...] = total.astype(bf16)
-
-
-def grad_pair(a0, a1, b0, b1):
-    width = b0.shape[1]
-    return kernel_call(
-        grad_pair_body,
+def feed_mine_body(
+    n_ref,
+    g_ref,
+    fc_ref,
+    proj_ref,
+    b_ref,
+    r_ref,
+    a_ref,
+    dh_ref,
+    m_ref,
+    dn_ref,
+    here_ref,
+    there_ref,
+    sum_ref,
+):
+    feed_core(n_ref, g_ref, fc_ref, proj_ref, b_ref, a_ref, dh_ref, sum_ref)
+    total = mm_nt(dh_ref[...], fc_ref[...]) + r_ref[...].astype(f32)
+    dn_ref[...] = total
+    parted(here_ref, there_ref, total.astype(bf16))
+    m_ref[...] = mm_nt(a_ref[...], proj_ref[...])
+
+
+def feed_mine(normed, cot, packed, fc_bias, dn_in):
+    return kernel_call(
+        feed_mine_body,
+        (2,),
+        [rows(D), rows(D), FC_COLUMNS, PROJ_COLUMNS, whole((1, D)), rows(D)],
+        [rows(D)] * 4 + [whole((BLK, D))] * 2 + [whole((8, D))],
+        [shape((HALF, D), bf16)] * 2
+        + [shape((HALF, D), f32)] * 2
+        + [shape((BLK, D), bf16)] * 2
+        + [shape((8, D), f32)],
+        8 * HALF * D * D,
+    )(normed, cot, packed, packed, fc_bias, dn_in)
+
+
+def feed_grads_body(n0_ref, n1_ref, h0_ref, h1_ref, g0_ref, g1_ref, a0_ref, a1_ref, o_ref):
+    o_ref[:, :D] = (mm_tn(n0_ref[...], h0_ref[...]) + mm_tn(n1_ref[...], h1_ref[...])).astype(bf16)
+    o_ref[:, D:] = (mm_tn(g0_ref[...], a0_ref[...]) + mm_tn(g1_ref[...], a1_ref[...])).astype(bf16)
+
+
+def feed_grads(n0, n1, h0, h1, g0, g1, a0, a1):
+    part = pl.BlockSpec((HALF, BLK), lambda i: (0, i))
+    full = whole((HALF, D))
+    return kernel_call(
+        feed_grads_body,
         (4,),
-        [pl.BlockSpec((HALF, BLK), lambda i: (0, i))] * 2 + [whole((HALF, width))] * 2,
-        rows(width),
-        shape((D, width), bf16),
-        2 * SEQ * D * width,
-    )(a0, a1, b0, b1)
-
-
-def mid_grad_body(s_ref, r_ref, mid_ref, g_ref, small_ref, dm_ref, low_ref, sum_ref):
-    d_normed = s_ref[...] + r_ref[...].astype(f32)
+        [part, part, full, full, part, part, full, full],
+        rows(2 * D),
+        shape((D, 2 * D), bf16),
+        4 * SEQ * D * D,
+    )(n0, n1, h0, h1, g0, g1, a0, a1)
+
+
+def mid_grad_body(
+    s_ref, here_ref, there_ref, mid_ref, g_ref, small_ref, dm_ref, low_ref, sum_ref
+):
+    d_normed = s_ref[...] + arrived(here_ref, there_ref)
     xhat, root = normalized(mid_ref[...])
     g = g_ref[...].astype(f32)
     d_middle = g + norm_pull(d_normed, xhat, root, small_ref[3:4, :])
@@ -343,15 +396,15 @@
         sum_ref[4:8, :] = jnp.zeros((4, D), f32)
 
 
-def mid_grad(s, r, middle, cot_mine, smalls):
+def mid_grad(s, here, there, middle, cot_mine, smalls):
     return kernel_call(
         mid_grad_body,
         (2,),
-        [rows(D), rows(D, lambda i: 1 - i), rows(D), rows(D), whole((8, D))],
+        [rows(D)] + [whole((BLK, D))] * 2 + [rows(D), rows(D), whole((8, D))],
         [rows(D), rows(D), whole((8, D))],
         [shape((HALF, D), f32), shape((HALF, D), bf16), shape((8, D), f32)],
         HALF * D * 20,
-    )(s, r, middle, cot_mine, smalls)
+    )(s, here, there, middle, cot_mine, smalls)
 
 
 def context_grad_body(d0_ref, d1_ref, w_ref, o_ref):
@@ -370,58 +423,95 @@
     )(d0, d1, packed)
 
 
-def norm_one_body(x_ref, q_ref, k_ref, v_ref, w_ref, o_ref, sum_ref):
-    partial = (
+def norm_one_body(q_ref, k_ref, v_ref, w_ref, o_ref):
+    o_ref[...] = (
         mm_nt(q_ref[...], w_ref[:, :256])
         + mm_nt(k_ref[...], w_ref[:, 256:512])
         + mm_nt(v_ref[...], w_ref[:, 512:768])
-    )
-    xhat, _ = normalized(x_ref[...].astype(f32))
-    o_ref[...] = partial.astype(bf16)
-
-    @pl.when(pl.program_id(0) == 0)
-    def _():
-        sum_ref[...] = jnp.zeros_like(sum_ref)
-
-    sum_ref[0:1, :] += jnp.sum(partial * xhat, axis=0, keepdims=True)
-    sum_ref[1:2, :] += jnp.sum(partial, axis=0, keepdims=True)
-    sum_ref[2:3, :256] += jnp.sum(q_ref[...].astype(f32), axis=0, keepdims=True)
-    sum_ref[2:3, 256:512] += jnp.sum(v_ref[...].astype(f32), axis=0, keepdims=True)
-
-
-def norm_one_rows(x_all, dq, dk, dv, packed):
+    ).astype(bf16)
+
+
+def norm_one_rows(dq, dk, dv, packed):
     return kernel_call(
         norm_one_body,
         (4,),
-        [rows(D), rows(256), rows(256), rows(256), whole((D, 896))],
-        [rows(D), whole((8, D))],
-        [shape((SEQ, D), bf16), shape((8, D), f32)],
+        [rows(256), rows(256), rows(256), whole((D, 768))],
+        rows(D),
+        shape((SEQ, D), bf16),
         2 * SEQ * D * 768,
-    )(x_all, dq, dk, dv, packed)
-
-
-def qkv_grad_body(n_ref, q_ref, k_ref, v_ref, o_ref):
+    )(dq, dk, dv, packed)
+
+
+def picked(vector, lane):
+    at = lax.broadcasted_iota(jnp.int32, (BLK, vector.shape[1]), 1)
+    return jnp.sum(jnp.where(at == lane, vector, 0.0), axis=1, keepdims=True)
+
+
+def attn_grads_body(
+    n_ref, q_ref, k_ref, v_ref, m0_ref, m1_ref, c_ref, w_ref, vec_ref, fc_ref, o_ref, sums
+):
+    step = pl.program_id(0)
+
+    @pl.when(step == 0)
+    def _():
+        for p, ref in enumerate((q_ref, k_ref, v_ref)):
+            sums[0:1, p * 256 : (p + 1) * 256] = jnp.sum(
+                ref[...].astype(f32), axis=0, keepdims=True
+            )
+
     n = n_ref[...]
-    o_ref[:, :256] = mm_tn(n, q_ref[...]).astype(bf16)
-    o_ref[:, 256:512] = mm_tn(n, k_ref[...]).astype(bf16)
-    o_ref[:, 512:768] = mm_tn(n, v_ref[...]).astype(bf16)
-
-
-def qkv_grad(normed, dq, dk, dv):
-    return kernel_call(
-        qkv_grad_body,
+    gain = w_ref[:, 1024:1025].astype(f32)
+    offset = w_ref[:, 1025:1026].astype(f32)
+    by_gain = jnp.zeros((BLK, 1), f32)
+    by_bias = jnp.zeros((BLK, 1), f32)
+    for p, ref in enumerate((q_ref, k_ref, v_ref)):
+        cut = slice(p * 256, (p + 1) * 256)
+        raw = mm_tn(n, ref[...])
+        total = sums[0:1, cut]
+        weight = w_ref[:, cut].astype(f32)
+        by_gain += jnp.sum(weight * raw, axis=1, keepdims=True)
+        by_bias += jnp.sum(weight * total, axis=1, keepdims=True)
+        o_ref[:, cut] = (raw * gain + offset * total).astype(bf16)
+    o_ref[:, 768:1024] = (
+        mm_tn(m0_ref[...], c_ref[:HALF, :]) + mm_tn(m1_ref[...], c_ref[HALF:, :])
+    ).astype(bf16)
+    row = lax.broadcasted_iota(jnp.int32, (BLK, 1), 0)
+    owner, inner = step * (BLK // 32) + row // 32, row % 32
+    columns = [by_gain, by_bias] + [picked(vec_ref[k : k + 1, :], row) for k in range(4)]
+    columns.append(picked(fc_ref[4:5, :], inner // 4 * 128 + owner * 4 + inner % 4))
+    lane = inner % 8 // 2 * HD + owner * 2 + inner % 2
+    from_q = picked(sums[0:1, 0:256], lane)
+    from_v = picked(sums[0:1, 512:768], lane)
+    columns.append(jnp.where(inner < 8, from_q, from_v))
+    at = lax.broadcasted_iota(jnp.int32, (BLK, 128), 1)
+    small = jnp.zeros((BLK, 128), f32)
+    for k, column in enumerate(columns):
+        small = jnp.where(at == k, column, small)
+    o_ref[:, 1024:1152] = small.astype(bf16)
+
+
+def attn_grads(xhat, dq, dk, dv, d_mid0, d_mid1, context, packed, vectors):
+    return kernel_call(
+        attn_grads_body,
         (4,),
-        [pl.BlockSpec((SEQ, BLK), lambda i: (0, i))] + [whole((SEQ, 256))] * 3,
-        rows(768),
-        shape((D, 768), bf16),
-        2 * SEQ * D * 768,
-    )(normed, dq, dk, dv)
-
-
-def input_grad_body(x_ref, a_ref, b_ref, c_ref, d_ref, dm_ref, small_ref, o_ref):
-    d_normed = (a_ref[...].astype(f32) + b_ref[...].astype(f32)) + (
-        c_ref[...].astype(f32) + d_ref[...].astype(f32)
-    )
+        [pl.BlockSpec((SEQ, BLK), lambda i: (0, i))]
+        + [whole((SEQ, 256))] * 3
+        + [pl.BlockSpec((HALF, BLK), lambda i: (0, i))] * 2
+        + [
+            whole((SEQ, 256)),
+            rows(1152),
+            pl.BlockSpec((8, BLK), lambda i: (0, i)),
+            whole((8, D)),
+        ],
+        rows(1152),
+        shape((D, 1152), bf16),
+        2 * SEQ * D * D,
+        scratch=[pltpu.VMEM((8, 768), f32)],
+    )(xhat, dq, dk, dv, d_mid0, d_mid1, context, packed, vectors, vectors)
+
+
+def input_grad_body(x_ref, a_ref, b_ref, c_ref, dm_ref, small_ref, o_ref):
+    d_normed = a_ref[...].astype(f32) + b_ref[...].astype(f32) + c_ref[...].astype(f32)
     xhat, root = normalized(x_ref[...].astype(f32))
     o_ref[...] = dm_ref[...] + norm_pull(d_normed, xhat, root, small_ref[0:1, :])
 
@@ -430,9 +520,16 @@
     return lax.ppermute(values, axis, SWAP)
 
 
-def to_owners(grad):
-    parts = lax.all_to_all(grad.reshape(32, 32, grad.shape[1]), DP, 0, 0, tiled=True)
-    return jnp.sum(parts.astype(f32), axis=0)
+def sent_to_owners(grad):
+    return lax.all_to_all(grad.reshape(16, 64, grad.shape[1]), XZ, 0, 0, tiled=True)
+
+
+def summed(parts):
+    total = jnp.sum(parts.astype(f32), axis=0)
+    yl = lax.axis_index("yl")
+    here = lax.dynamic_slice_in_dim(total, yl * 32, 32, 0)
+    there = lax.dynamic_slice_in_dim(total, (1 - yl) * 32, 32, 0)
+    return here + swap(there.astype(bf16), "yl").astype(f32)
 
 
 def shards(
@@ -466,113 +563,112 @@
         ],
         axis=1,
     )
-    first_pack = jnp.concatenate(
-        [w_qkv.reshape(32, 768), jnp.pad(tiny, ((0, 0), (0, 120)))], axis=1
-    )
-    packed_qkv = lax.all_to_all(
-        jnp.broadcast_to(first_pack, (32, 32, 896)), DP, 0, 0, tiled=True
-    ).reshape(D, 896)
-    second_pack = jnp.concatenate([w_fc, w_proj.T, w_out.T], axis=1)
-    neighbour = swap(second_pack, "yl")
+    pack = jnp.concatenate(
+        [w_qkv.reshape(32, 768), w_out.T, jnp.pad(tiny, ((0, 0), (0, 120))), w_fc, w_proj.T],
+        axis=1,
+    )
+    neighbour = swap(pack, "yl")
     both = jnp.where(
-        yl == 0,
-        jnp.concatenate([second_pack, neighbour]),
-        jnp.concatenate([neighbour, second_pack]),
-    )
-    packed = lax.all_gather(both, ("x", "z"), axis=0, tiled=True)
-
+        yl == 0, jnp.concatenate([pack, neighbour]), jnp.concatenate([neighbour, pack])
+    )
+    packed_attn = lax.all_to_all(
+        jnp.broadcast_to(both[:, :1152], (16, 64, 1152)), XZ, 0, 0, tiled=True
+    ).reshape(D, 1152)
+    small_t = packed_attn[:, 1024:1032].T
+    at = jnp.arange(4, dtype=jnp.int32)
+    loc = (at // 2 != yh).astype(jnp.int32) + 2 * (at % 2 != core).astype(jnp.int32)
+    segc, segr = segments.reshape(SEQ, 1), segments.reshape(1, SEQ)
     x_mine = jnp.concatenate([tokens, swap(tokens, "yh")])
     x_all = jnp.concatenate([x_mine, swap(x_mine, "core")])
-    cot_mine = jnp.concatenate([cotangent, swap(cotangent, "yh")])
-    cot_other = swap(cot_mine, "core")
-
-    small_t = packed_qkv[:, 768:776].T
+    second, small_t, x_all, segc = lax.optimization_barrier(
+        (both[:, 1152:], small_t, x_all, segc)
+    )
+    packed = lax.all_gather(second, XZ, axis=0, tiled=True)
+
     smalls = small_t.astype(f32)
     qv = small_t[6].reshape(32, 32)[:, :16].reshape(32, 2, 4, 2).transpose(1, 2, 0, 3)
     qv = qv.reshape(2, 256).astype(f32)
     bias_row = jnp.concatenate([qv[0], jnp.zeros((256,), f32), qv[1]])[None]
     fc_bias = small_t[7].reshape(32, 8, 4).transpose(1, 0, 2).reshape(1, D).astype(f32)
 
-    at = jnp.arange(4, dtype=jnp.int32)
-    loc = (at // 2 != yh).astype(jnp.int32) + 2 * (at % 2 != core).astype(jnp.int32)
-    segc, segr = segments.reshape(SEQ, 1), segments.reshape(1, SEQ)
-
-    normed_one, joined = qkv_rows(x_all, packed_qkv, smalls, bias_row)
+    xhat_one, joined = qkv_rows(x_all, packed_attn, smalls, bias_row)
+    joined, cot_late = lax.optimization_barrier((joined, cotangent))
+    cot_mine = jnp.concatenate([cotangent, swap(cot_late, "yh")])
+    cot_other = swap(cot_mine, "core")
     context = attend_forward(loc, segc, segr, joined)
-    received = swap(out_other(context, packed), "core")
-    s_out, s_out_low = out_mine(context, packed, received)
-    middle, n2_mine = middle_rows(x_mine, s_out, swap(s_out_low, "yh"), smalls)
+    context, cot_mine = lax.optimization_barrier((context, cot_mine))
+    received = swap(out_other(context, packed_attn), "core")
+    s_out, out_here, out_there = out_mine(context, packed_attn, received)
+    middle, n2_mine = middle_rows(
+        x_mine, s_out, swap(out_there, "yh"), swap(out_here, "yh"), smalls
+    )
     n2_other = swap(n2_mine, "core")
 
-    act0, dh0, mlp0, dn0, sum0 = feed_rows(n2_mine, cot_mine, packed, fc_bias, f32)
-    act1, dh1, mlp1, dn1, sum1 = feed_rows(n2_other, cot_other, packed, fc_bias, bf16)
-    s_dn = dn0 + swap(dn1, "core").astype(f32)
-    r_dn = swap(s_dn.astype(bf16), "yh")
-    s_mlp = mlp0 + swap(mlp1, "core").astype(f32)
-    r_mlp = swap(s_mlp[BLK:].astype(bf16), "yh")
+    act1, dh1, mlp1, dn1, sum1 = feed_other(n2_other, cot_other, packed, fc_bias)
+    dn_in = swap(dn1, "core")
+    act0, dh0, mlp0, s_dn, dn_here, dn_there, sum0 = feed_mine(
+        n2_mine, cot_mine, packed, fc_bias, dn_in
+    )
+    from_there, from_here = swap(dn_there, "yh"), swap(dn_here, "yh")
+    ff_grads = feed_grads(n2_mine, n2_other, dh0, dh1, cot_mine, cot_other, act0, act1)
+    ff_grads, from_there = lax.optimization_barrier((ff_grads, from_there))
+    ff_parts = sent_to_owners(ff_grads)
+    d_middle, d_mid0, mid_sums = mid_grad(
+        s_dn, from_there, from_here, middle, cot_mine, smalls
+    )
+    d_mid1 = swap(d_mid0, "core")
+    d_context = context_grad(d_mid0, d_mid1, packed_attn)
+
+    mlp1, _ = lax.optimization_barrier((mlp1, mid_sums))
+    mlp_in = swap(mlp1, "core")
+    mlp_there = (mlp0[BLK:] + mlp_in[BLK:].astype(f32)).astype(bf16)
+    r_mlp = swap(mlp_there, "yh").astype(f32)
     mixed = (
-        middle[:BLK] + (s_mlp[:BLK] + r_mlp.astype(f32)) + smalls[5:6]
+        middle[:BLK] + (mlp0[:BLK] + mlp_in[:BLK].astype(f32) + r_mlp) + smalls[5:6]
     ).astype(bf16)
-    grad_fc = to_owners(grad_pair(n2_mine, n2_other, dh0, dh1))
-    grad_proj = to_owners(grad_pair(cot_mine, cot_other, act0, act1)).T
-
-    d_middle, d_mid0, mid_sums = mid_grad(s_dn, r_dn, middle, cot_mine, smalls)
-    d_mid1 = swap(d_mid0, "core")
-    d_context = context_grad(d_mid0, d_mid1, packed)
-    grad_out = to_owners(grad_pair(d_mid0, d_mid1, context[:HALF], context[HALF:])).T
-
+    vectors = jnp.concatenate([mid_sums[0:4], sum0[0:1] + sum1[0:1], mid_sums[5:8]])
     dq, dk, dv = attend_backward(loc, segc, segr, joined, d_context)
-    grad_qkv = to_owners(qkv_grad(normed_one, dq, dk, dv)).reshape(32, 3, 256)
-    d_n1, one_sums = norm_one_rows(x_all, dq, dk, dv, packed_qkv)
+    grads = attn_grads(xhat_one, dq, dk, dv, d_mid0, d_mid1, context, packed_attn, vectors)
+    grads, dq, dk, dv = lax.optimization_barrier((grads, dq, dk, dv))
+    grads, ff_parts, mixed = lax.optimization_barrier((grads, ff_parts, mixed))
+    grad_attn = summed(sent_to_owners(grads))
+    grad_ff = summed(ff_parts)
+    grad_fc, grad_proj = grad_ff[:, :D], grad_ff[:, D:].T
+    grad_qkv, grad_out = grad_attn[:, :768].reshape(32, 3, 256), grad_attn[:, 768:1024].T
+    d_n1 = norm_one_rows(dq, dk, dv, packed_attn)
     from_core = swap(d_n1[HALF:], "core")
     s_n1 = d_n1[BLK:HALF].astype(f32) + from_core[BLK:].astype(f32)
     from_far = swap(s_n1.astype(bf16), "yh")
     input_grad = kernel_call(
         input_grad_body,
         (1,),
-        [whole((BLK, D))] * 2
-        + [whole((BLK, D))] * 4
-        + [whole((8, D))],
+        [whole((BLK, D))] * 5 + [whole((8, D))],
         whole((BLK, D)),
         shape((BLK, D), f32),
         BLK * D * 20,
-    )(
-        tokens,
-        d_n1[:BLK],
-        from_core[:BLK],
-        from_far,
-        jnp.zeros_like(from_far),
-        d_middle[:BLK],
-        smalls,
-    )
-
-    mine = (jnp.arange(4) == 2 * yh + core).astype(f32)[None, :, None]
-    norms = jnp.concatenate([one_sums[0:2], mid_sums[0:2]]).reshape(4, 32, 4, 8)
-    biases = mid_sums[2:4].reshape(2, 32, 1, 32)
-    fc_sum = (sum0[0] + sum1[0]).reshape(8, 32, 4).transpose(1, 0, 2).reshape(32, 1, 32)
-    qv_sum = one_sums[2, :512].reshape(2, 4, 32, 2).transpose(2, 0, 1, 3).reshape(32, 1, 16)
-    small_out = jnp.concatenate(
-        [norms[0], norms[1], norms[2], norms[3]]
-        + [jnp.broadcast_to(biases[k], (32, 4, 32)) for k in range(2)]
-        + [fc_sum * mine, qv_sum * mine, jnp.zeros((32, 4, 112), f32)],
-        axis=2,
-    ).reshape(128, 1, 256)
-    small_in = jnp.sum(lax.all_to_all(small_out, ALL, 0, 0, tiled=True), axis=(0, 1))
+    )(tokens, d_n1[:BLK], from_core[:BLK], from_far, d_middle[:BLK], smalls)
+
+    small = grad_attn[:, 1024:1032]
+    turned = [
+        lax.ppermute(small, TP, [(k, (k + turn) % 4) for k in range(4)]) for turn in (1, 2, 3)
+    ]
+    everywhere = small + turned[0] + (turned[1] + turned[2])
+    share = lax.dynamic_slice_in_dim(everywhere, 8 * (2 * yh + core), 8, 0)
     return (
         mixed,
         input_grad,
-        small_in[0:8],
-        small_in[8:16],
+        share[:, 0],
+        share[:, 1],
         grad_qkv,
-        small_in[128:144].reshape(2, 4, 2),
+        small[:16, 7].reshape(2, 4, 2),
         grad_out,
-        small_in[64:96],
-        small_in[16:24],
-        small_in[24:32],
+        everywhere[:, 5],
+        share[:, 2],
+        share[:, 3],
         grad_fc,
-        small_in[96:128].reshape(8, 4),
+        small[:, 6].reshape(8, 4),
         grad_proj,
-        small_in[32:64],
+        everywhere[:, 4],
     )
 
 

time: 365 us -> 305 us (0.84)
  waiting for transfers between devices: 142 us -> 97.7 us
  starting transfers between devices: 59.1 us -> 42.8 us
  Pallas kernels: 87.4 us -> 100 us
  other arithmetic: 23.7 us -> 13.6 us
    all_to_all x6 -> x3, starting transfers between devices: 42.4 us -> 19.5 us  [the longest x2 11.4 us: sent_to_owners(): lax.all_to_all(grad.reshape(16, 64, grad.shape[1]), XZ, 0, 0, tiled=True)]
    all_to_all x6 -> x3, waiting for transfers between devices: 45 us -> 22.3 us  [the longest x1 11.2 us: shards(): lax.all_to_all(jnp.broadcast_to(both[:, :1152], (16, 64, 1152)), XZ, 0, 0...]
    all_gather x1, waiting for transfers between devices: 14.1 us -> 0.01 us  [shards(): packed = lax.all_gather(second, XZ, axis=0, tiled=True)]
    ppermute x15 -> x19, waiting for transfers between devices: 83.1 us -> 74.1 us  [swap(): return lax.ppermute(values, axis, SWAP)]
    pallas_call x11 -> x9, Pallas kernels: 56.9 us -> 63.3 us  [the longest x1 10.6 us: feed_mine(): kernel_call(feed_mine_body, (2,), [rows(D), rows(D), FC_COLUMNS, PROJ_COL...]
    concatenate x7 -> x3, local copies, waits for them, and re-layouts: 8 us -> 1.71 us  [the longest x1 0.84 us: shards(): jnp.concatenate([w_qkv.reshape(32, 768), w_out.T, jnp.pad(tiny, ((0, 0),...]
    reduce_sum x5 -> x2, other arithmetic: 8.91 us -> 3.32 us  [summed(): total = jnp.sum(parts.astype(f32), axis=0)]
    convert_element_type x4 -> x2, other arithmetic: 6.68 us -> 2.2 us  [the longest x1 1.14 us: shards(): mixed = (middle[:BLK] + (mlp0[:BLK] + mlp_in[:BLK].astype(f32) + r_mlp) +...]
  transfers between devices with their start and end apart: 22 -> 26, of which waited for: 13 -> 15; matrix products, arithmetic and copies ran while one was open for 13% -> 11% of each run, Pallas kernels for 20% -> 26%
where the time goes in v2:
time: 305 us; the launch traced here: 304 us
  Pallas kernels  100 us (33%)
  waiting for transfers between devices  97.7 us (32%)
  starting transfers between devices  42.8 us (14%)
  local copies, waits for them, and re-layouts  35.1 us (12%)
  between operations  14.3 us (5%)
  other arithmetic  13.6 us (4%)
    ppermute x19, waiting for transfers between devices, swap(): return lax.ppermute(values, axis, SWAP)  74.1 us
    ppermute x19, starting transfers between devices, swap(): return lax.ppermute(values, axis, SWAP)  19.4 us
    pallas_call x1, Pallas kernels, attend_backward(): kernel_call(attend_back_body, (2,), [whole((SEQ, 1)), whole((1, SEQ)), co...  15.8 us
    unnamed x52, local copies, waits for them, and re-layouts  11.9 us
    pallas_call x1, Pallas kernels, attend_forward(): kernel_call(attend_body, (2,), [whole((SEQ, 1)), whole((1, SEQ)), column_...  11.4 us
    all_to_all x2, starting transfers between devices, sent_to_owners(): lax.all_to_all(grad.reshape(16, 64, grad.shape[1]), XZ, 0, 0, tiled=True)  11.4 us
    all_to_all x1, waiting for transfers between devices, shards(): lax.all_to_all(jnp.broadcast_to(both[:, :1152], (16, 64, 1152)), XZ, 0, 0...  11.2 us
    all_to_all x2, waiting for transfers between devices, sent_to_owners(): lax.all_to_all(grad.reshape(16, 64, grad.shape[1]), XZ, 0, 0, tiled=True)  11.2 us
  transfers between devices with their start and end apart: 26, of which 15 were waited for; matrix products, arithmetic and copies ran while one was open for 11% of the time, Pallas kernels for 26%

profile of v2, /device:TPU:0, one launch (start us, length us, event | category | flops | bytes accessed | tf_op | source)
XLA Modules:
  0.0 303.7 jit_solution(11617545449277023203)
XLA Ops:
  9.8 0.8 copy.88
  11.3 0.8 constant_dynamic-update-slice_fusion
  12.2 0.8 bitcast_dynamic-update-slice_fusion
  13.0 1.7 collective-permute-start
  14.7 5.1 %collective-permute-done = bf16[32,3200]{1,0:T(8,128)(2,1)S(1)} collective-permute-done((bf16[32,3200]{1,0:T(8,128)(2,1)S(1)}, bf16[32,3200]{1,0:T(8,128)(2,1)S(1)}, u32[]{:S(2)}, u32[]{:S(2)}) %collective-permute-start) | collective-permute-done | bytes 204832 | tf_op jit(solution)/shard_map/ppermute | solution.py:520
  20.6 1.8 broadcast_in_dim.9
  22.3 8.2 %all-to-all-start = ((bf16[16,64,1152]{2,1,0:T(8,128)(2,1)}), bf16[16,64,1152]{2,1,0:T(8,128)(2,1)S(1)}, u32[]{:S(2)}, u32[]{:S(2)}) async-start(bf16[16,64,1152]{2,1,0:T(8,128)(2,1)} %broadcast_in_dim.9), calls=%async_computation | async-start | bytes 4718592 | tf_op jit(solution)/shard_map/all_to_all | solution.py:574
  30.6 3.3 %collective-permute-start.1 = (bf16[256,1024]{1,0:T(8,128)(2,1)S(1)}, bf16[256,1024]{1,0:T(8,128)(2,1)S(1)}, u32[]{:S(2)}, u32[]{:S(2)}) collective-permute-start(bf16[256,1024]{1,0:T(8,128)(2,1)S(1)} %copy-done.2), channel_id=1, source_target_pairs={{0,2},{2,0},{1,3},{3,1},{4,6},{6,4},{5,7},{7,5},{8,10},{10,8},{9,1... | collective-permute-start | bytes 1572872 | tf_op jit(solution)/shard_map/ppermute | solution.py:520
  33.9 0.8 constant_dynamic-update-slice_fusion.5
  34.7 10.0 %collective-permute-done.1 = bf16[256,1024]{1,0:T(8,128)(2,1)S(1)} collective-permute-done((bf16[256,1024]{1,0:T(8,128)(2,1)S(1)}, bf16[256,1024]{1,0:T(8,128)(2,1)S(1)}, u32[]{:S(2)}, u32[]{:S(2)}) %collective-permute-start.1) | collective-permute-done | bytes 524320 | tf_op jit(solution)/shard_map/ppermute | solution.py:520
  44.7 0.8 constant_dynamic-update-slice_fusion.4.x_ref
  46.3 2.3 collective-permute-done.2
  48.5 2.8 pad_maximum_fusion.x_ref
  51.3 11.2 %all-to-all-done = bf16[16,64,1152]{2,1,0:T(8,128)(2,1)S(1)} async-done(((bf16[16,64,1152]{2,1,0:T(8,128)(2,1)}), bf16[16,64,1152]{2,1,0:T(8,128)(2,1)S(1)}, u32[]{:S(2)}, u32[]{:S(2)}) %all-to-all-start) | async-done | bytes 2359328 | tf_op jit(solution)/shard_map/all_to_all | solution.py:574
  62.7 0.9 convert_element_type.72.small_ref
  64.9 6.2 %shard_map.254 = (bf16[1024,1024]{1,0:T(8,128)(2,1)}, bf16[1024,768]{1,0:T(8,128)(2,1)}) custom-call(bf16[1024,1024]{1,0:T(8,128)(2,1)} %pad_maximum_fusion.x_ref, bf16[1024,1152]{1,0:T(8,128)(2,1)} %bitcast.40, f32[8,1024]{1,0:T(8,128)} %convert_element_type.72.small_ref, f32[1,768]{1,0:T(1,128)} %broadcast_in_dim.11.bias_ref), custom_call_target="tpu_custom_call" | custom-call | flops 1610612736 | bytes 8388608 | tf_op jit(solution)/shard_map/pallas_call | solution.py:93
  71.0 3.2 %collective-permute-start.3 = (bf16[256,1024]{1,0:T(8,128)(2,1)S(1)}, bf16[256,1024]{1,0:T(8,128)(2,1)S(1)}, u32[]{:S(2)}, u32[]{:S(2)}) collective-permute-start(bf16[256,1024]{1,0:T(8,128)(2,1)S(1)} %copy-done.13), channel_id=1, source_target_pairs={{0,2},{2,0},{1,3},{3,1},{4,6},{6,4},{5,7},{7,5},{8,10},{10,8},{9,1... | collective-permute-start | bytes 1572872 | tf_op jit(solution)/shard_map/ppermute | solution.py:520
  74.8 1.0 copy.81.segc_ref
  75.9 11.4 %shard_map.255.c_ref = bf16[1024,256]{1,0:T(8,128)(2,1)} custom-call(s32[4]{0:T(128)} %fusion.loc_ref, s32[1024,1]{1,0:T(8,128)} %copy.81.segc_ref, s32[1,1024]{1,0:T(1,128)} %bitcast.57, bf16[1024,768]{1,0:T(8,128)(2,1)} %get-tuple-element.62.q_ref.k_ref.v_ref, bf16[1024,768]{1,0:T(8,128)(2,1)} %get-tuple-element.62.q_ref.k_ref.v_ref, ...), custom_call_target="tpu_custom_call" | custom-call | flops 1073741824 | bytes 8388608 | tf_op jit(solution)/shard_map/pallas_call | solution.py:144
  87.3 3.0 shard_map.256
  90.3 2.9 collective-permute-done.4.r_ref
  93.1 1.0 copy-done.10
  94.1 3.5 %shard_map.257 = (f32[512,1024]{1,0:T(8,128)}, bf16[256,1024]{1,0:T(8,128)(2,1)}, bf16[256,1024]{1,0:T(8,128)(2,1)}) custom-call(bf16[1024,256]{1,0:T(8,128)(2,1)} %shard_map.255.c_ref, bf16[1024,1152]{1,0:T(8,128)(2,1)} %bitcast.42, bf16[512,1024]{1,0:T(8,128)(2,1)} %copy-done.10), custom_call_target="tpu_custom_call" | custom-call | flops 268435456 | bytes 8388608 | tf_op jit(solution)/shard_map/pallas_call | solution.py:252
  97.9 3.2 %collective-permute-start.6 = (bf16[256,1024]{1,0:T(8,128)(2,1)}, bf16[256,1024]{1,0:T(8,128)(2,1)S(1)}, u32[]{:S(2)}, u32[]{:S(2)}) collective-permute-start(bf16[256,1024]{1,0:T(8,128)(2,1)} %get-tuple-element.67), channel_id=1, source_target_pairs={{0,2},{2,0},{1,3},{3,1},{4,6},{6,4},{5,7},{7,5},{8,10},{10,8},{9,1... | collective-permute-start | bytes 1572872 | tf_op jit(solution)/shard_map/ppermute | solution.py:520
  101.1 12.9 %collective-permute-done.5.here_ref = bf16[256,1024]{1,0:T(8,128)(2,1)S(1)} collective-permute-done((bf16[256,1024]{1,0:T(8,128)(2,1)}, bf16[256,1024]{1,0:T(8,128)(2,1)S(1)}, u32[]{:S(2)}, u32[]{:S(2)}) %collective-permute-start.5) | collective-permute-done | bytes 524320 | tf_op jit(solution)/shard_map/ppermute | solution.py:520
  114.1 10.4 %collective-permute-done.6.there_ref = bf16[256,1024]{1,0:T(8,128)(2,1)S(1)} collective-permute-done((bf16[256,1024]{1,0:T(8,128)(2,1)}, bf16[256,1024]{1,0:T(8,128)(2,1)S(1)}, u32[]{:S(2)}, u32[]{:S(2)}) %collective-permute-start.6) | collective-permute-done | bytes 524320 | tf_op jit(solution)/shard_map/ppermute | solution.py:520
  124.5 0.8 copy-done.15
  125.4 3.6 %shard_map.258 = (f32[512,1024]{1,0:T(8,128)}, bf16[512,1024]{1,0:T(8,128)(2,1)}) custom-call(bf16[512,1024]{1,0:T(8,128)(2,1)} %constant_dynamic-update-slice_fusion.4.x_ref, f32[512,1024]{1,0:T(8,128)} %get-tuple-element.65.s_ref, bf16[256,1024]{1,0:T(8,128)(2,1)} %copy-done.14, bf16[256,1024]{1,0:T(8,128)(2,1)} %copy-done.15, ...), custom_call_target="tpu_custom_call" | custom-call | flops 5242880 | bytes 8388608 | tf_op jit(solution)/shard_map/pallas_call | solution.py:275
  129.9 2.1 collective-permute-done.7.n_ref.n1_ref
  131.9 9.3 %shard_map.259 = (bf16[512,1024]{1,0:T(8,128)(2,1)}, bf16[512,1024]{1,0:T(8,128)(2,1)}, bf16[512,1024]{1,0:T(8,128)(2,1)}, bf16[512,1024]{1,0:T(8,128)(2,1)}, f32[8,1024]{1,0:T(8,128)}) custom-call(bf16[512,1024]{1,0:T(8,128)(2,1)} %collective-permute-done.7.n_ref.n1_ref, bf16[512,1024]{1,0:T(8,128)(2,1)} %copy-done.17, ...), custom_call_target="tpu_custom_call" | custom-call | flops 4294967296 | bytes 8388608 | tf_op jit(solution)/shard_map/pallas_call | solution.py:315
  141.4 2.8 collective-permute-done.9.r_ref
  144.1 1.1 copy-done.18
  145.2 10.6 %shard_map.260 = (bf16[512,1024]{1,0:T(8,128)(2,1)}, bf16[512,1024]{1,0:T(8,128)(2,1)}, f32[512,1024]{1,0:T(8,128)}, f32[512,1024]{1,0:T(8,128)}, bf16[256,1024]...) custom-call(bf16[512,1024]{1,0:T(8,128)(2,1)} %get-tuple-element.68.n_ref.n0_ref, ...), custom_call_target="tpu_custom_call" | custom-call | flops 4294967296 | bytes 8388608 | tf_op jit(solution)/shard_map/pallas_call | solution.py:348
  156.2 9.1 %shard_map.261 = bf16[1024,2048]{1,0:T(8,128)(2,1)} custom-call(bf16[512,1024]{1,0:T(8,128)(2,1)} %get-tuple-element.68.n_ref.n0_ref, bf16[512,1024]{1,0:T(8,128)(2,1)} %collective-permute-done.7.n_ref.n1_ref, bf16[512,1024]{1,0:T(8,128)(2,1)} %get-tuple-element.73.h0_ref, bf16[512,1024]{1,0:T(8,128)(2,1)} %get-tuple-element.74.h1_ref, ...), custom_call_target="tpu_custom_call" | custom-call | flops 4294967296 | bytes 8388608 | tf_op jit(solution)/shard_map/pallas_call | solution.py:369
  165.3 6.3 %collective-permute-done.10.here_ref = bf16[256,1024]{1,0:T(8,128)(2,1)S(1)} collective-permute-done((bf16[256,1024]{1,0:T(8,128)(2,1)}, bf16[256,1024]{1,0:T(8,128)(2,1)S(1)}, u32[]{:S(2)}, u32[]{:S(2)}) %collective-permute-start.10) | collective-permute-done | bytes 524320 | tf_op jit(solution)/shard_map/ppermute | solution.py:520
  171.6 0.8 copy-done.11
  172.4 4.5 %all-to-all-start.1 = ((bf16[16,64,2048]{2,1,0:T(8,128)(2,1)}), bf16[16,64,2048]{2,1,0:T(8,128)(2,1)}, u32[]{:S(2)}, u32[]{:S(2)}) async-start(bf16[16,64,2048]{2,1,0:T(8,128)(2,1)} %bitcast.47), calls=%async_computation.1 | async-start | bytes 8388608 | tf_op jit(solution)/shard_map/all_to_all | solution.py:524
  177.3 14.4 %collective-permute-done.11.there_ref = bf16[256,1024]{1,0:T(8,128)(2,1)S(1)} collective-permute-done((bf16[256,1024]{1,0:T(8,128)(2,1)S(1)}, bf16[256,1024]{1,0:T(8,128)(2,1)S(1)}, u32[]{:S(2)}, u32[]{:S(2)}) %collective-permute-start.11) | collective-permute-done | bytes 524320 | tf_op jit(solution)/shard_map/ppermute | solution.py:520
  191.7 0.8 copy-done.12
  192.5 5.9 %shard_map.262 = (f32[512,1024]{1,0:T(8,128)}, bf16[512,1024]{1,0:T(8,128)(2,1)}, f32[8,1024]{1,0:T(8,128)}) custom-call(f32[512,1024]{1,0:T(8,128)} %get-tuple-element.72.s_ref, bf16[256,1024]{1,0:T(8,128)(2,1)} %copy-done.11, bf16[256,1024]{1,0:T(8,128)(2,1)} %copy-done.12, f32[512,1024]{1,0:T(8,128)} %get-tuple-element.80.mid_ref, ...), custom_call_target="tpu_custom_call" | custom-call | flops 10485760 | bytes 8388608 | tf_op jit(solution)/shard_map/pallas_call | solution.py:400
  202.0 1.1 add_convert_fusion.2
  203.4 1.0 copy-done.3
  204.4 3.2 %shard_map.263.d_ref = bf16[1024,256]{1,0:T(8,128)(2,1)} custom-call(bf16[512,1024]{1,0:T(8,128)(2,1)} %get-tuple-element.81.d0_ref.m0_ref, bf16[512,1024]{1,0:T(8,128)(2,1)} %copy-done.3, bf16[1024,1152]{1,0:T(8,128)(2,1)} %bitcast.43), custom_call_target="tpu_custom_call" | custom-call | flops 536870912 | bytes 8388608 | tf_op jit(solution)/shard_map/pallas_call | solution.py:416
  207.6 15.8 %shard_map.264 = (bf16[1024,256]{1,0:T(8,128)(2,1)}, bf16[1024,256]{1,0:T(8,128)(2,1)}, bf16[1024,256]{1,0:T(8,128)(2,1)}) custom-call(s32[4]{0:T(128)} %fusion.loc_ref, s32[1024,1]{1,0:T(8,128)} %copy.81.segc_ref, s32[1,1024]{1,0:T(1,128)} %bitcast.58, bf16[1024,768]{1,0:T(8,128)(2,1)} %get-tuple-element.62.q_ref.k_ref.v_ref, ...), custom_call_target="tpu_custom_call" | custom-call | flops 2684354560 | bytes 8388608 | tf_op jit(solution)/shard_map/pallas_call | solution.py:196
  223.4 9.3 %shard_map.265 = bf16[1024,1152]{1,0:T(8,128)(2,1)} custom-call(bf16[1024,1024]{1,0:T(8,128)(2,1)} %get-tuple-element.59.n_ref, bf16[1024,256]{1,0:T(8,128)(2,1)} %get-tuple-element.94.q_ref, bf16[1024,256]{1,0:T(8,128)(2,1)} %get-tuple-element.95.k_ref, bf16[1024,256]{1,0:T(8,128)(2,1)} %get-tuple-element.96.v_ref, ...), custom_call_target="tpu_custom_call" | custom-call | flops 2147483648 | bytes 8388608 | tf_op jit(solution)/shard_map/pallas_call | solution.py:494
  232.7 5.7 %shard_map.266 = bf16[1024,1024]{1,0:T(8,128)(2,1)} custom-call(bf16[1024,256]{1,0:T(8,128)(2,1)} %get-tuple-element.94.q_ref, bf16[1024,256]{1,0:T(8,128)(2,1)} %get-tuple-element.95.k_ref, bf16[1024,256]{1,0:T(8,128)(2,1)} %get-tuple-element.96.v_ref, bf16[1024,1152]{1,0:T(8,128)(2,1)} %bitcast.45), custom_call_target="tpu_custom_call" | custom-call | flops 1610612736 | bytes 8388608 | tf_op jit(solution)/shard_map/pallas_call | solution.py:435
  238.3 2.4 slice.162
  240.8 1.1 add_convert_fusion.1
  241.9 6.8 %all-to-all-start.2 = ((bf16[16,64,1152]{2,1,0:T(8,128)(2,1)}), bf16[16,64,1152]{2,1,0:T(8,128)(2,1)S(1)}, u32[]{:S(2)}, u32[]{:S(2)}) async-start(bf16[16,64,1152]{2,1,0:T(8,128)(2,1)} %bitcast.46), calls=%async_computation.2 | async-start | bytes 4718592 | tf_op jit(solution)/shard_map/all_to_all | solution.py:524
  248.8 1.4 add_convert_fusion
  250.2 3.3 %collective-permute-start.16 = (bf16[256,1024]{1,0:T(8,128)(2,1)S(1)}, bf16[256,1024]{1,0:T(8,128)(2,1)}, u32[]{:S(2)}, u32[]{:S(2)}) collective-permute-start(bf16[256,1024]{1,0:T(8,128)(2,1)S(1)} %add_convert_fusion), channel_id=1, source_target_pairs={{0,2},{2,0},{1,3},{3,1},{4,6},{6,4},{5,7},{7,5},{8,10},{10,8},{9,1... | collective-permute-start | bytes 1572872 | tf_op jit(solution)/shard_map/ppermute | solution.py:520
  253.5 3.0 convert_reduce_fusion
  256.6 1.0 collective-permute-start.21
  257.5 2.3 slice.138.dm_ref
  259.9 1.9 slice.161.a_ref
  261.7 1.9 slice.163.b_ref
  263.6 3.0 collective-permute-done.16.c_ref
  266.6 3.7 %shard_map.267 = f32[256,1024]{1,0:T(8,128)} custom-call(bf16[256,1024]{1,0:T(8,128)(2,1)} %x_ref.1, bf16[256,1024]{1,0:T(8,128)(2,1)} %slice.161.a_ref, bf16[256,1024]{1,0:T(8,128)(2,1)} %slice.163.b_ref, bf16[256,1024]{1,0:T(8,128)(2,1)} %collective-permute-done.16.c_ref, f32[256,1024]{1,0:T(8,128)} %slice.138.dm_ref, f32[8,1024]{1,0:T(8,128)} %convert_element_type.72.small_ref), custom_call_target="tpu_custom_call" | custom-call | flops 5242880 | bytes 8388608 | tf_op jit(solution)/shard_map/pallas_call | solution.py:642
  270.3 0.9 convert_add_fusion
  271.2 11.2 %all-to-all-done.2 = bf16[16,64,1152]{2,1,0:T(8,128)(2,1)S(1)} async-done(((bf16[16,64,1152]{2,1,0:T(8,128)(2,1)}), bf16[16,64,1152]{2,1,0:T(8,128)(2,1)S(1)}, u32[]{:S(2)}, u32[]{:S(2)}) %all-to-all-start.2) | async-done | bytes 2359328 | tf_op jit(solution)/shard_map/all_to_all | solution.py:524
  282.7 1.7 collective-permute-start.17
  285.2 2.0 collective-permute-done.17
  287.4 3.3 %collective-permute-start.19 = (f32[32,8]{1,0:T(8,128)S(1)}, f32[32,8]{1,0:T(8,128)S(1)}, u32[]{:S(2)}, u32[]{:S(2)}) collective-permute-start(f32[32,8]{1,0:T(8,128)S(1)} %slice.166), channel_id=1, source_target_pairs={{0,2},{1,3},{2,0},{3,1},{4,6},{5,7},{6,4},{7,5},{8,10},{9,11},{10,... | collective-permute-start | bytes 3080 | tf_op jit(solution)/shard_map/ppermute | solution.py:653
  294.2 1.2 collective-permute-done.18
  (118 shorter events, 19.1 us)
Async XLA Ops:
  13.0 6.7 %collective-permute-start = (bf16[32,3200]{1,0:T(8,128)(2,1)S(1)}, bf16[32,3200]{1,0:T(8,128)(2,1)S(1)}, u32[]{:S(2)}, u32[]{:S(2)}) collective-permute-start(bf16[32,3200]{1,0:T(8,128)(2,1)S(1)} %bitcast_dynamic-update-slice_fusion), channel_id=1, source_target_pairs={{0,4},{4,0},{1,5},{5,1},{2,6},{6,2},{3,7},{7,3},{8,12},{12,8},{9,1... | collective-permute-start | bytes 614408 | tf_op jit(solution)/shard_map/ppermute | solution.py:520
  19.8 0.8 copy-start.6
  22.3 8.2 %copy-start.2 = (bf16[256,1024]{1,0:T(8,128)(2,1)S(1)}, bf16[256,1024]{1,0:T(8,128)(2,1)}, u32[]{:S(2)}) copy-start(bf16[256,1024]{1,0:T(8,128)(2,1)} %x_ref.1) | copy-start | bytes 1572868
  22.3 40.1 %all-to-all-start = ((bf16[16,64,1152]{2,1,0:T(8,128)(2,1)}), bf16[16,64,1152]{2,1,0:T(8,128)(2,1)S(1)}, u32[]{:S(2)}, u32[]{:S(2)}) async-start(bf16[16,64,1152]{2,1,0:T(8,128)(2,1)} %broadcast_in_dim.9), calls=%async_computation | async-start | bytes 4718592 | tf_op jit(solution)/shard_map/all_to_all | solution.py:574
  30.5 101.4 %all-gather.2.cloned.1.call-start = ((), (), s32[]{:S(2)}) async-start(), calls=%async_computation.3 | async-start | bytes 4456448 | tf_op jit(solution)/shard_map/all_gather | solution.py:586
  30.6 14.9 %copy-start.7 = (bf16[64,3200]{1,0:T(8,128)(2,1)S(1)}, bf16[64,3200]{1,0:T(8,128)(2,1)}, u32[]{:S(2)}) copy-start(bf16[64,3200]{1,0:T(8,128)(2,1)} %copy-done.6) | copy-start | bytes 1228804
  30.6 14.1 %collective-permute-start.1 = (bf16[256,1024]{1,0:T(8,128)(2,1)S(1)}, bf16[256,1024]{1,0:T(8,128)(2,1)S(1)}, u32[]{:S(2)}, u32[]{:S(2)}) collective-permute-start(bf16[256,1024]{1,0:T(8,128)(2,1)S(1)} %copy-done.2), channel_id=1, source_target_pairs={{0,2},{2,0},{1,3},{3,1},{4,6},{6,4},{5,7},{7,5},{8,10},{10,8},{9,1... | collective-permute-start | bytes 1572872 | tf_op jit(solution)/shard_map/ppermute | solution.py:520
  45.5 3.0 collective-permute-start.2
  62.5 2.4 copy-start
  64.9 6.2 %copy-start.13 = (bf16[256,1024]{1,0:T(8,128)(2,1)S(1)}, bf16[256,1024]{1,0:T(8,128)(2,1)}, u32[]{:S(2)}) copy-start(bf16[256,1024]{1,0:T(8,128)(2,1)} %param.16) | copy-start | bytes 1572868
  64.9 10.0 %copy-start.16 = (s32[1024]{0:T(1024)S(1)}, s32[1024]{0:T(1024)}, u32[]{:S(2)}) copy-start(s32[1024]{0:T(1024)} %param.17) | copy-start | bytes 12292
  71.0 16.2 %collective-permute-start.3 = (bf16[256,1024]{1,0:T(8,128)(2,1)S(1)}, bf16[256,1024]{1,0:T(8,128)(2,1)S(1)}, u32[]{:S(2)}, u32[]{:S(2)}) collective-permute-start(bf16[256,1024]{1,0:T(8,128)(2,1)S(1)} %copy-done.13), channel_id=1, source_target_pairs={{0,2},{2,0},{1,3},{3,1},{4,6},{6,4},{5,7},{7,5},{8,10},{10,8},{9,1... | collective-permute-start | bytes 1572872 | tf_op jit(solution)/shard_map/ppermute | solution.py:520
  87.3 13.9 %copy-start.4 = (bf16[512,1024]{1,0:T(8,128)(2,1)}, bf16[512,1024]{1,0:T(8,128)(2,1)S(1)}, u32[]{:S(2)}) copy-start(bf16[512,1024]{1,0:T(8,128)(2,1)S(1)} %constant_dynamic-update-slice_fusion.6.g_ref.g0_ref) | copy-start | bytes 3145732
  90.3 2.9 collective-permute-start.4
  93.1 1.0 copy-start.10
  97.6 16.5 %collective-permute-start.5 = (bf16[256,1024]{1,0:T(8,128)(2,1)}, bf16[256,1024]{1,0:T(8,128)(2,1)S(1)}, u32[]{:S(2)}, u32[]{:S(2)}) collective-permute-start(bf16[256,1024]{1,0:T(8,128)(2,1)} %get-tuple-element.66), channel_id=1, source_target_pairs={{0,2},{2,0},{1,3},{3,1},{4,6},{6,4},{5,7},{7,5},{8,10},{10,8},{9,1... | collective-permute-start | bytes 1572872 | tf_op jit(solution)/shard_map/ppermute | solution.py:520
  97.9 26.6 %collective-permute-start.6 = (bf16[256,1024]{1,0:T(8,128)(2,1)}, bf16[256,1024]{1,0:T(8,128)(2,1)S(1)}, u32[]{:S(2)}, u32[]{:S(2)}) collective-permute-start(bf16[256,1024]{1,0:T(8,128)(2,1)} %get-tuple-element.67), channel_id=1, source_target_pairs={{0,2},{2,0},{1,3},{3,1},{4,6},{6,4},{5,7},{7,5},{8,10},{10,8},{9,1... | collective-permute-start | bytes 1572872 | tf_op jit(solution)/shard_map/ppermute | solution.py:520
  101.1 28.7 %collective-permute-start.8 = (bf16[512,1024]{1,0:T(8,128)(2,1)S(1)}, bf16[512,1024]{1,0:T(8,128)(2,1)S(1)}, u32[]{:S(2)}, u32[]{:S(2)}) collective-permute-start(bf16[512,1024]{1,0:T(8,128)(2,1)S(1)} %constant_dynamic-update-slice_fusion.6.g_ref.g0_ref), channel_id=1, source_target_pairs={{0,1},{1,0},{2,3},{3,2},{4,5},{5,4},{6,7},{7,6},{8,9},{9,8},{10,11... | collective-permute-start | bytes 3145736 | tf_op jit(solution)/shard_map/ppermute | solution.py:520
  114.1 10.4 %copy-start.14 = (bf16[256,1024]{1,0:T(8,128)(2,1)}, bf16[256,1024]{1,0:T(8,128)(2,1)S(1)}, u32[]{:S(2)}) copy-start(bf16[256,1024]{1,0:T(8,128)(2,1)S(1)} %collective-permute-done.5.here_ref) | copy-start | bytes 1572868
  124.5 0.9 copy-start.15
  128.9 3.0 collective-permute-start.7
  129.9 2.1 copy-start.17
  141.3 2.9 collective-permute-start.9
  144.1 1.1 copy-start.18
  155.8 15.8 %collective-permute-start.10 = (bf16[256,1024]{1,0:T(8,128)(2,1)}, bf16[256,1024]{1,0:T(8,128)(2,1)S(1)}, u32[]{:S(2)}, u32[]{:S(2)}) collective-permute-start(bf16[256,1024]{1,0:T(8,128)(2,1)} %get-tuple-element.77), channel_id=1, source_target_pairs={{0,2},{2,0},{1,3},{3,1},{4,6},{6,4},{5,7},{7,5},{8,10},{10,8},{9,1... | collective-permute-start | bytes 1572872 | tf_op jit(solution)/shard_map/ppermute | solution.py:520
  171.6 0.8 copy-start.11
  171.6 5.4 %copy-start.19 = (bf16[256,1024]{1,0:T(8,128)(2,1)S(1)}, bf16[256,1024]{1,0:T(8,128)(2,1)}, u32[]{:S(2)}) copy-start(bf16[256,1024]{1,0:T(8,128)(2,1)} %get-tuple-element.79) | copy-start | bytes 1572868
  172.4 69.6 %all-to-all-start.1 = ((bf16[16,64,2048]{2,1,0:T(8,128)(2,1)}), bf16[16,64,2048]{2,1,0:T(8,128)(2,1)}, u32[]{:S(2)}, u32[]{:S(2)}) async-start(bf16[16,64,2048]{2,1,0:T(8,128)(2,1)} %bitcast.47), calls=%async_computation.1 | async-start | bytes 8388608 | tf_op jit(solution)/shard_map/all_to_all | solution.py:524
  176.9 14.7 %collective-permute-start.11 = (bf16[256,1024]{1,0:T(8,128)(2,1)S(1)}, bf16[256,1024]{1,0:T(8,128)(2,1)S(1)}, u32[]{:S(2)}, u32[]{:S(2)}) collective-permute-start(bf16[256,1024]{1,0:T(8,128)(2,1)S(1)} %copy-done.19), channel_id=1, source_target_pairs={{0,2},{2,0},{1,3},{3,1},{4,6},{6,4},{5,7},{7,5},{8,10},{10,8},{9,1... | collective-permute-start | bytes 1572872 | tf_op jit(solution)/shard_map/ppermute | solution.py:520
  191.7 0.8 copy-start.12
  192.5 9.5 %copy-start.5 = (f32[512,1024]{1,0:T(8,128)S(1)}, f32[512,1024]{1,0:T(8,128)}, u32[]{:S(2)}) copy-start(f32[512,1024]{1,0:T(8,128)} %get-tuple-element.90) | copy-start | bytes 6291460
  198.4 3.5 %collective-permute-start.13 = (bf16[512,1024]{1,0:T(8,128)(2,1)}, bf16[512,1024]{1,0:T(8,128)(2,1)S(1)}, u32[]{:S(2)}, u32[]{:S(2)}) collective-permute-start(bf16[512,1024]{1,0:T(8,128)(2,1)} %get-tuple-element.92), channel_id=1, source_target_pairs={{0,1},{1,0},{2,3},{3,2},{4,5},{5,4},{6,7},{7,6},{8,9},{9,8},{10,11... | collective-permute-start | bytes 3145736 | tf_op jit(solution)/shard_map/ppermute | solution.py:520
  198.5 4.9 %collective-permute-start.12 = (bf16[512,1024]{1,0:T(8,128)(2,1)}, bf16[512,1024]{1,0:T(8,128)(2,1)S(1)}, u32[]{:S(2)}, u32[]{:S(2)}) collective-permute-start(bf16[512,1024]{1,0:T(8,128)(2,1)} %get-tuple-element.81.d0_ref.m0_ref), channel_id=1, source_target_pairs={{0,1},{1,0},{2,3},{3,2},{4,5},{5,4},{6,7},{7,6},{8,9},{9,8},{10,11... | collective-permute-start | bytes 3145736 | tf_op jit(solution)/shard_map/ppermute | solution.py:520
  202.0 1.1 copy-start.8
  203.1 37.7 %collective-permute-start.14 = (bf16[256,1024]{1,0:T(8,128)(2,1)}, bf16[256,1024]{1,0:T(8,128)(2,1)S(1)}, u32[]{:S(2)}, u32[]{:S(2)}) collective-permute-start(bf16[256,1024]{1,0:T(8,128)(2,1)} %add_convert_fusion.2), channel_id=1, source_target_pairs={{0,2},{2,0},{1,3},{3,1},{4,6},{6,4},{5,7},{7,5},{8,10},{10,8},{9,1... | collective-permute-start | bytes 1572872 | tf_op jit(solution)/shard_map/ppermute | solution.py:520
  203.4 1.0 copy-start.3
  232.7 8.1 %copy-start.9 = (bf16[512,1024]{1,0:T(8,128)(2,1)S(1)}, bf16[512,1024]{1,0:T(8,128)(2,1)}, u32[]{:S(2)}) copy-start(bf16[512,1024]{1,0:T(8,128)(2,1)} %copy-done.8) | copy-start | bytes 3145732
  238.3 2.5 copy-start.1
  240.8 8.0 %collective-permute-start.15 = (bf16[512,1024]{1,0:T(8,128)(2,1)}, bf16[512,1024]{1,0:T(8,128)(2,1)}, u32[]{:S(2)}, u32[]{:S(2)}) collective-permute-start(bf16[512,1024]{1,0:T(8,128)(2,1)} %slice.162), channel_id=1, source_target_pairs={{0,1},{1,0},{2,3},{3,2},{4,5},{5,4},{6,7},{7,6},{8,9},{9,8},{10,11... | collective-permute-start | bytes 3145736 | tf_op jit(solution)/shard_map/ppermute | solution.py:520
  241.9 40.4 %all-to-all-start.2 = ((bf16[16,64,1152]{2,1,0:T(8,128)(2,1)}), bf16[16,64,1152]{2,1,0:T(8,128)(2,1)S(1)}, u32[]{:S(2)}, u32[]{:S(2)}) async-start(bf16[16,64,1152]{2,1,0:T(8,128)(2,1)} %bitcast.46), calls=%async_computation.2 | async-start | bytes 4718592 | tf_op jit(solution)/shard_map/all_to_all | solution.py:524
  250.2 16.4 %collective-permute-start.16 = (bf16[256,1024]{1,0:T(8,128)(2,1)S(1)}, bf16[256,1024]{1,0:T(8,128)(2,1)}, u32[]{:S(2)}, u32[]{:S(2)}) collective-permute-start(bf16[256,1024]{1,0:T(8,128)(2,1)S(1)} %add_convert_fusion), channel_id=1, source_target_pairs={{0,2},{2,0},{1,3},{3,1},{4,6},{6,4},{5,7},{7,5},{8,10},{10,8},{9,1... | collective-permute-start | bytes 1572872 | tf_op jit(solution)/shard_map/ppermute | solution.py:520
  256.6 13.7 %collective-permute-start.21 = (bf16[32,2048]{1,0:T(8,128)(2,1)S(1)}, bf16[32,2048]{1,0:T(8,128)(2,1)}, u32[]{:S(2)}, u32[]{:S(2)}) collective-permute-start(bf16[32,2048]{1,0:T(8,128)(2,1)S(1)} %dynamic-slice_convert_fusion), channel_id=1, source_target_pairs={{0,4},{4,0},{1,5},{5,1},{2,6},{6,2},{3,7},{7,3},{8,12},{12,8},{9,1... | collective-permute-start | bytes 393224 | tf_op jit(solution)/shard_map/ppermute | solution.py:520
  282.7 4.4 %collective-permute-start.17 = (bf16[32,1152]{1,0:T(8,128)(2,1)S(1)}, bf16[32,1152]{1,0:T(8,128)(2,1)S(1)}, u32[]{:S(2)}, u32[]{:S(2)}) collective-permute-start(bf16[32,1152]{1,0:T(8,128)(2,1)S(1)} %dynamic-slice_convert_fusion.1), channel_id=1, source_target_pairs={{0,4},{4,0},{1,5},{5,1},{2,6},{6,2},{3,7},{7,3},{8,12},{12,8},{9,1... | collective-permute-start | bytes 221192 | tf_op jit(solution)/shard_map/ppermute | solution.py:520
  287.4 6.8 %collective-permute-start.19 = (f32[32,8]{1,0:T(8,128)S(1)}, f32[32,8]{1,0:T(8,128)S(1)}, u32[]{:S(2)}, u32[]{:S(2)}) collective-permute-start(f32[32,8]{1,0:T(8,128)S(1)} %slice.166), channel_id=1, source_target_pairs={{0,2},{1,3},{2,0},{3,1},{4,6},{5,7},{6,4},{7,5},{8,10},{9,11},{10,... | collective-permute-start | bytes 3080 | tf_op jit(solution)/shard_map/ppermute | solution.py:653
  290.7 3.5 %collective-permute-start.20 = (f32[32,8]{1,0:T(8,128)S(1)}, f32[32,8]{1,0:T(8,128)S(1)}, u32[]{:S(2)}, u32[]{:S(2)}) collective-permute-start(f32[32,8]{1,0:T(8,128)S(1)} %slice.166), channel_id=1, source_target_pairs={{0,3},{1,0},{2,1},{3,2},{4,7},{5,4},{6,5},{7,6},{8,11},{9,8},{10,9... | collective-permute-start | bytes 3080 | tf_op jit(solution)/shard_map/ppermute | solution.py:653
  290.7 4.7 %collective-permute-start.18 = (f32[32,8]{1,0:T(8,128)S(1)}, f32[32,8]{1,0:T(8,128)S(1)}, u32[]{:S(2)}, u32[]{:S(2)}) collective-permute-start(f32[32,8]{1,0:T(8,128)S(1)} %slice.166), channel_id=1, source_target_pairs={{0,1},{1,2},{2,3},{3,0},{4,5},{5,6},{6,7},{7,4},{8,9},{9,10},{10,1... | collective-permute-start | bytes 3080 | tf_op jit(solution)/shard_map/ppermute | solution.py:653
Sparse Core Ops, SparseCore 0:
  62.8 50.2 all-gather.1
